TPU v7x, 128 devices: a whole 4x4x4 slice. The times are simulated.
128 devices in a mesh: section: 8 (over y, core), dp: 8 (over z_hi, x), tensor: 2 (over z_lo).
Axes of the slice: x: 4, y: 4, z: 4 (z_hi: 2, z_lo: 2; z = z_hi * 2 + z_lo), core: 2. Of those that a mesh axis runs over, the one named last changes fastest.
Arguments:
- states_in: bfloat16 [2, 8, 128, 3584], P(None, 'section', ('dp', 'tensor')), may hold values from -40 to 40
- entering: bfloat16 [1, 2, 128, 3584], P(None, None, ('dp', 'tensor')), may hold values from -40 to 40
- saved: bfloat16 [2, 2, 8, 128, 3584], P(None, None, 'section', ('dp', 'tensor')), may hold values from -40 to 40
- cotangent: bfloat16 [2, 8, 128, 3584], P(None, 'section', ('dp', 'tensor')), may hold values from -1.5 to 1.5
- cot_entering: bfloat16 [1, 2, 128, 3584], P(None, None, ('dp', 'tensor')), may hold values from -1.5 to 1.5
- gains: bfloat16 [8, 3584], replicated, may hold values from 0.5 to 1.5
- up_rows: bfloat16 [8, 2, 9216, 3584], P('section', None, ('dp', 'tensor')), may hold values from -1 to 1, as said below
- down_rows: bfloat16 [8, 2, 9216, 3584], P('section', None, ('dp', 'tensor')), may hold values from -1 to 1, as said below
Outputs:
- states_out: bfloat16 [2, 2, 8, 128, 3584], P(None, None, 'section', ('dp', 'tensor'))
- input_grads: bfloat16 [2, 2, 8, 128, 3584], P(None, None, 'section', ('dp', 'tensor'))
- grad_up: bfloat16 [8, 9216, 3584], P('section', ('dp', 'tensor'))
- grad_down: bfloat16 [8, 9216, 3584], P('section', ('dp', 'tensor'))
Inputs may be any that keep to these rules, and one draw needn't show every extreme that they name: up_rows[s, 1] equals up_rows[7 - s, 0] for every section s: both slots hold copies of a layer. down_rows[s, 1] equals down_rows[7 - s, 0] for every section s: both slots hold copies of a layer.
All inputs are finite; a program needn't handle non-finite values.
Results may differ from a plain program's by a relative error of at most 0.007.
Values may be sent and summed in bfloat16 or wider, within the bound.
A program may use at most 128 MiB of HBM per device.

v0:
```python
import jax
import jax.numpy as jnp
from jax import lax
from jax.sharding import PartitionSpec as P

EPSILON = 1e-06


def for_sending(array):

    def short(part):
        return part.astype(jnp.bfloat16) if part.dtype == jnp.float32 else part

    return jax.tree.map(short, array)


def shifted(block, axis, distance):
    devices = range(lax.axis_size(axis))
    route = [(i - distance, i) for i in devices if i - distance in devices]
    return lax.ppermute(block, axis, route)


def contract_last(former, latter):
    return lax.dot_general(
        former, latter, (((1,), (1,)), ((), ())), preferred_element_type=jnp.float32
    )


def contract_first(former, latter):
    return lax.dot_general(
        former, latter, (((0,), (0,)), ((), ())), preferred_element_type=jnp.float32
    )


def normalize(states, scaling):
    widened = states.astype(jnp.float32)
    factor = lax.rsqrt(jnp.mean(widened * widened, axis=-1, keepdims=True) + EPSILON)
    normed = (widened * factor * scaling).astype(jnp.bfloat16)
    return (widened, factor, normed)


def norm_back(widened, factor, scaling, upstream, d_normed):
    scaled = d_normed * scaling
    unit_rows = widened * factor
    d_norm = factor * (scaled - unit_rows * jnp.mean(unit_rows * scaled, axis=-1, keepdims=True))
    return (upstream.astype(jnp.float32) + d_norm).astype(jnp.bfloat16)


def split_rows(members, sections):
    return tuple(
        (
            member.reshape((sections, member.shape[0] // sections) + member.shape[1:])
            for member in members
        )
    )


def merge_rows(members):
    return tuple((member.reshape((-1,) + member.shape[2:]) for member in members))


def mirror_finished(members, sections):
    blocks = split_rows(members, sections)
    for rounds in range(2):
        if rounds == 1:
            blocks = tuple((jnp.flip(member, 0) for member in blocks))
        blocks = jax.tree.map(
            lambda part, own: part.astype(own.dtype),
            lax.all_to_all(for_sending(blocks), "section", split_axis=0, concat_axis=0, tiled=True),
            blocks,
        )
    return merge_rows(blocks)


def body(states_in, entering, saved, cotangent, cot_entering, gains, up_rows, down_rows):
    sections = lax.axis_size("section")
    position = lax.axis_index("section")
    at_first = position == 0
    at_last = position == sections - 1
    forward_gain = lax.dynamic_index_in_dim(gains, position, 0, keepdims=False).astype(jnp.float32)
    mirror_gain = lax.dynamic_index_in_dim(
        gains, sections - 1 - position, 0, keepdims=False
    ).astype(jnp.float32)
    group_gain = (forward_gain, mirror_gain)
    up_pair = (up_rows[0, 0], up_rows[0, 1])
    down_pair = (down_rows[0, 0], down_rows[0, 1])
    features = states_in.shape[-1]
    periods = saved.shape[0]
    inflow = (states_in[0, 0], states_in[1, 0])
    upstream = (cotangent[0, 0], cotangent[1, 0])
    produced_all = []
    returned_all = []
    stored = ([], [])
    for period in range(periods):
        leading = [normalize(inflow[course], group_gain[course]) for course in range(2)]
        trailing = [normalize(saved[period, course, 0], group_gain[course]) for course in range(2)]
        gathered = (
            lax.all_gather(leading[0][2], ("dp", "tensor"), axis=0, tiled=True),
            lax.all_gather(leading[1][2], ("dp", "tensor"), axis=0, tiled=True),
            lax.all_gather(trailing[0][2], ("dp", "tensor"), axis=0, tiled=True),
            lax.all_gather(upstream[0], ("dp", "tensor"), axis=0, tiled=True),
            lax.all_gather(trailing[1][2], ("dp", "tensor"), axis=0, tiled=True),
            lax.all_gather(upstream[1], ("dp", "tensor"), axis=0, tiled=True),
        )
        activated = [
            jax.nn.silu(contract_last(gathered[course], up_pair[course])).astype(jnp.bfloat16)
            for course in range(2)
        ]
        slopes = []
        for course in range(2):
            normed_all = gathered[2 + 2 * course]
            upstream_all = gathered[3 + 2 * course]
            hidden = contract_last(normed_all, up_pair[course])
            gating = jax.nn.sigmoid(hidden)
            d_hidden = (
                contract_last(upstream_all, down_pair[course])
                * gating
                * (1.0 + hidden * (1.0 - gating))
            ).astype(jnp.bfloat16)
            stored[course].append(
                (normed_all, upstream_all, jax.nn.silu(hidden).astype(jnp.bfloat16), d_hidden)
            )
            slopes.append(d_hidden)

        def combine():
            terms_list = [
                jnp.dot(activated[course], down_pair[course], preferred_element_type=jnp.float32)
                for course in range(2)
            ]
            terms_list = terms_list + [
                jnp.dot(slopes[course], up_pair[course], preferred_element_type=jnp.float32)
                for course in range(2)
            ]
            return jnp.concatenate(terms_list, axis=1)

        summed = lax.psum_scatter(combine(), ("dp", "tensor"), scatter_dimension=0, tiled=True)
        produced = [
            (leading[course][0] + summed[:, course * features : (course + 1) * features]).astype(
                jnp.bfloat16
            )
            for course in range(2)
        ]
        returned = [
            norm_back(
                trailing[course][0],
                trailing[course][1],
                group_gain[course],
                upstream[course],
                summed[:, (2 + course) * features : (3 + course) * features],
            )
            for course in range(2)
        ]
        produced_all.append(jnp.stack(produced)[:, None])
        returned_all.append(jnp.stack(returned)[:, None])
        if period + 1 < periods:
            onward = shifted(jnp.stack([produced[0], returned[1]]), "section", 1)
            backward = shifted(jnp.stack([produced[1], returned[0]]), "section", -1)
            inflow = (
                jnp.where(at_first, entering[period, 0], onward[0]),
                jnp.where(at_last, entering[period, 1], backward[0]),
            )
            upstream = (
                jnp.where(at_last, cot_entering[period, 0], backward[1]),
                jnp.where(at_first, cot_entering[period, 1], onward[1]),
            )
    near_terms = tuple((jnp.concatenate(members, axis=0) for members in zip(*stored[0])))
    far_terms = tuple((jnp.concatenate(members, axis=0) for members in zip(*stored[1])))
    near_up = contract_first(near_terms[3], near_terms[0])
    near_down = contract_first(near_terms[2], near_terms[1])
    local_up = contract_first(far_terms[3], far_terms[0]).astype(jnp.bfloat16)
    local_down = contract_first(far_terms[2], far_terms[1]).astype(jnp.bfloat16)
    mirrored = mirror_finished((local_up, local_down), sections)
    mirror_up = mirrored[0].astype(jnp.float32)
    mirror_down = mirrored[1].astype(jnp.float32)
    grad_up = (near_up + mirror_up).astype(jnp.bfloat16)[None]
    grad_down = (near_down + mirror_down).astype(jnp.bfloat16)[None]
    return (jnp.stack(produced_all), jnp.stack(returned_all), grad_up, grad_down)


def solution(mesh):
    placed = (
        P(None, "section", ("dp", "tensor"), None),
        P(None, None, ("dp", "tensor"), None),
        P(None, None, "section", ("dp", "tensor"), None),
        P(None, "section", ("dp", "tensor"), None),
        P(None, None, ("dp", "tensor"), None),
        P(),
        P("section", None, ("dp", "tensor"), None),
        P("section", None, ("dp", "tensor"), None),
    )
    return jax.shard_map(
        body,
        mesh=mesh,
        in_specs=placed,
        out_specs=(
            P(None, None, "section", ("dp", "tensor"), None),
            P(None, None, "section", ("dp", "tensor"), None),
            P("section", ("dp", "tensor"), None),
            P("section", ("dp", "tensor"), None),
        ),
        check_vma=False,
    )
```

profile of v0, /device:TPU:1, one launch (start us, length us, event | category | flops | bytes accessed | tf_op | source)
XLA Modules:
  0.0 953.2 jit_solution(13497368728647251217)
XLA Ops:
  11.3 39.9 %all_gather.41 = bf16[128,3584]{1,0:T(8,128)(2,1)S(1)} all-gather(bf16[8,3584]{1,0:T(8,128)(2,1)S(1)} %get-tuple-element.52), channel_id=1, replica_groups=mesh['section'=8,'dp'=8,'tensor'=2] {'dp','tensor'}, dimensions={0}, use_global_device_ids=true | all-gather | bytes 974848 | tf_op jit(solution)/shard_map/all_gather | solution.py:102
  52.1 34.5 %all-gather.1 = bf16[1,1,128,3584]{3,2,1,0:T(8,128)(2,1)S(1)} all-gather(bf16[1,1,8,3584]{3,2,1,0:T(8,128)(2,1)S(1)} %get-tuple-element.47), channel_id=3, replica_groups=mesh['section'=8,'dp'=8,'tensor'=2] {'dp','tensor'}, dimensions={2}, use_global_device_ids=true | all-gather | bytes 974848 | tf_op jit(solution)/shard_map/all_gather | solution.py:103
  86.6 4.5 multiply_convert_fusion.1
  94.1 33.3 %all_gather.39 = bf16[128,3584]{1,0:T(8,128)(2,1)S(1)} all-gather(bf16[8,3584]{1,0:T(8,128)(2,1)S(1)} %get-tuple-element.53), channel_id=1, replica_groups=mesh['section'=8,'dp'=8,'tensor'=2] {'dp','tensor'}, dimensions={0}, use_global_device_ids=true | all-gather | bytes 974848 | tf_op jit(solution)/shard_map/all_gather | solution.py:100
  129.3 35.3 %all-gather = bf16[1,1,128,3584]{3,2,1,0:T(8,128)(2,1)S(1)} all-gather(bf16[1,1,8,3584]{3,2,1,0:T(8,128)(2,1)S(1)} %get-tuple-element.46), channel_id=2, replica_groups=mesh['section'=8,'dp'=8,'tensor'=2] {'dp','tensor'}, dimensions={2}, use_global_device_ids=true | all-gather | bytes 974848 | tf_op jit(solution)/shard_map/all_gather | solution.py:101
  168.0 35.5 %all_gather.37 = bf16[128,3584]{1,0:T(8,128)(2,1)} all-gather(bf16[8,3584]{1,0:T(8,128)(2,1)S(1)} %get-tuple-element.45), channel_id=1, replica_groups=mesh['section'=8,'dp'=8,'tensor'=2] {'dp','tensor'}, dimensions={0}, use_global_device_ids=true | all-gather | bytes 974848 | tf_op jit(solution)/shard_map/all_gather | solution.py:99
  203.5 8.4 fusion.10
  211.8 35.8 %all_gather.36 = bf16[128,3584]{1,0:T(8,128)(2,1)} all-gather(bf16[8,3584]{1,0:T(8,128)(2,1)S(1)} %get-tuple-element.44), channel_id=1, replica_groups=mesh['section'=8,'dp'=8,'tensor'=2] {'dp','tensor'}, dimensions={0}, use_global_device_ids=true | all-gather | bytes 974848 | tf_op jit(solution)/shard_map/all_gather | solution.py:98
  247.7 8.4 fusion.30
  256.1 4.9 pad_maximum_fusion
  261.1 193.1 %reduce-scatter.3.cloned.1.call-done = f32[8,14336]{1,0:T(8,128)} async-done(((f32[128,14336]{1,0:T(8,128)}), f32[8,14336]{1,0:T(8,128)}) %reduce-scatter.3.cloned.1.call-update) | async-done | bytes 458768 | tf_op jit(solution)/shard_map/reduce_scatter | solution.py:136
  463.4 40.6 %all_gather.47 = bf16[128,3584]{1,0:T(8,128)(2,1)S(1)} all-gather(bf16[8,3584]{1,0:T(8,128)(2,1)S(1)} %get-tuple-element.36), channel_id=1, replica_groups=mesh['section'=8,'dp'=8,'tensor'=2] {'dp','tensor'}, dimensions={0}, use_global_device_ids=true | all-gather | bytes 974848 | tf_op jit(solution)/shard_map/all_gather | solution.py:102
  508.1 34.7 %all_gather.45 = bf16[128,3584]{1,0:T(8,128)(2,1)S(1)} all-gather(bf16[8,3584]{1,0:T(8,128)(2,1)S(1)} %get-tuple-element.37), channel_id=1, replica_groups=mesh['section'=8,'dp'=8,'tensor'=2] {'dp','tensor'}, dimensions={0}, use_global_device_ids=true | all-gather | bytes 974848 | tf_op jit(solution)/shard_map/all_gather | solution.py:100
  542.8 4.6 multiply_convert_fusion.2
  547.4 35.5 %all_gather.46 = bf16[128,3584]{1,0:T(8,128)(2,1)S(1)} all-gather(bf16[8,3584]{1,0:T(8,128)(2,1)S(1)} %get-tuple-element.43), channel_id=1, replica_groups=mesh['section'=8,'dp'=8,'tensor'=2] {'dp','tensor'}, dimensions={0}, use_global_device_ids=true | all-gather | bytes 974848 | tf_op jit(solution)/shard_map/all_gather | solution.py:103
  589.4 35.5 %all_gather.44 = bf16[128,3584]{1,0:T(8,128)(2,1)} all-gather(bf16[8,3584]{1,0:T(8,128)(2,1)S(1)} %get-tuple-element.42), channel_id=1, replica_groups=mesh['section'=8,'dp'=8,'tensor'=2] {'dp','tensor'}, dimensions={0}, use_global_device_ids=true | all-gather | bytes 974848 | tf_op jit(solution)/shard_map/all_gather | solution.py:101
  624.9 31.1 %all-to-all-start = ((bf16[8,72,3584]{2,1,0:T(8,128)(2,1)}), bf16[8,72,3584]{2,1,0:T(8,128)(2,1)}, u32[]{:S(2)}, u32[]{:S(2)}) async-start(bf16[8,72,3584]{2,1,0:T(8,128)(2,1)} %bitcast.222), calls=%async_computation.2 | async-start | bytes 8257536 | tf_op jit(solution)/shard_map/all_to_all | solution.py:69
  657.2 37.9 %all_gather.42 = bf16[128,3584]{1,0:T(8,128)(2,1)} all-gather(bf16[8,3584]{1,0:T(8,128)(2,1)S(1)} %fusion.188), channel_id=1, replica_groups=mesh['section'=8,'dp'=8,'tensor'=2] {'dp','tensor'}, dimensions={0}, use_global_device_ids=true | all-gather | bytes 974848 | tf_op jit(solution)/shard_map/all_gather | solution.py:98
  695.1 8.4 fusion.26
  703.6 36.3 %all_gather.43 = bf16[128,3584]{1,0:T(8,128)(2,1)} all-gather(bf16[8,3584]{1,0:T(8,128)(2,1)S(1)} %fusion.192), channel_id=1, replica_groups=mesh['section'=8,'dp'=8,'tensor'=2] {'dp','tensor'}, dimensions={0}, use_global_device_ids=true | all-gather | bytes 974848 | tf_op jit(solution)/shard_map/all_gather | solution.py:99
  739.9 8.4 fusion.6
  759.9 4.2 convolution_convert_fusion
  764.1 17.2 %all-to-all-start.2 = ((bf16[8,72,3584]{2,1,0:T(8,128)(2,1)}), bf16[8,72,3584]{2,1,0:T(8,128)(2,1)}, u32[]{:S(2)}, u32[]{:S(2)}) async-start(bf16[8,72,3584]{2,1,0:T(8,128)(2,1)} %bitcast.223), calls=%async_computation.4 | async-start | bytes 8257536 | tf_op jit(solution)/shard_map/all_to_all | solution.py:69
  781.3 4.5 rev.7
  785.7 43.8 %all-to-all-done.2 = bf16[8,72,3584]{2,1,0:T(8,128)(2,1)} async-done(((bf16[8,72,3584]{2,1,0:T(8,128)(2,1)}), bf16[8,72,3584]{2,1,0:T(8,128)(2,1)}, u32[]{:S(2)}, u32[]{:S(2)}) %all-to-all-start.2) | async-done | bytes 4128800 | tf_op jit(solution)/shard_map/all_to_all | solution.py:69
  829.5 5.3 all-to-all-start.1
  834.8 4.4 rev.8
  839.2 43.8 %all-to-all-done.1 = bf16[8,72,3584]{2,1,0:T(8,128)(2,1)} async-done(((bf16[8,72,3584]{2,1,0:T(8,128)(2,1)}), bf16[8,72,3584]{2,1,0:T(8,128)(2,1)}, u32[]{:S(2)}, u32[]{:S(2)}) %all-to-all-start.1) | async-done | bytes 4128800 | tf_op jit(solution)/shard_map/all_to_all | solution.py:69
  883.1 5.3 all-to-all-start.3
  888.4 5.4 fusion.2
  893.8 42.8 %all-to-all-done.3 = bf16[8,72,3584]{2,1,0:T(8,128)(2,1)} async-done(((bf16[8,72,3584]{2,1,0:T(8,128)(2,1)}), bf16[8,72,3584]{2,1,0:T(8,128)(2,1)}, u32[]{:S(2)}, u32[]{:S(2)}) %all-to-all-start.3) | async-done | bytes 4128800 | tf_op jit(solution)/shard_map/all_to_all | solution.py:69
  936.6 5.9 fusion.3
  (109 shorter events, 49.7 us)
Async XLA Ops:
  7.2 447.0 %reduce-scatter.3.cloned.1.call-start = ((), (), s32[]{:S(2)}) async-start(), calls=%async_computation.6 | async-start | bytes 7798784 | tf_op jit(solution)/shard_map/reduce_scatter | solution.py:136
  51.2 39.9 %copy-start.7 = (bf16[128,3584]{1,0:T(8,128)(2,1)}, bf16[128,3584]{1,0:T(8,128)(2,1)S(1)}, u32[]{:S(2)}) copy-start(bf16[128,3584]{1,0:T(8,128)(2,1)S(1)} %all_gather.41) | copy-start | bytes 2752516
  52.1 39.0 %copy-start.21 = (bf16[1,2,576,3584]{3,2,1,0:T(8,128)(2,1)S(1)}, bf16[1,2,576,3584]{3,2,1,0:T(8,128)(2,1)}, u32[]{:S(2)}) copy-start(bf16[1,2,576,3584]{3,2,1,0:T(8,128)(2,1)} %param.15) | copy-start | bytes 24772612
  86.6 5.7 copy-start.5
  86.6 5.7 slice-start
  127.4 37.2 %copy-start = (bf16[128,3584]{1,0:T(8,128)(2,1)}, bf16[128,3584]{1,0:T(8,128)(2,1)S(1)}, u32[]{:S(2)}) copy-start(bf16[128,3584]{1,0:T(8,128)(2,1)S(1)} %all_gather.39) | copy-start | bytes 2752516
  261.0 193.1 %copy-start.4 = (bf16[2,2,1,8,3584]{4,3,2,1,0:T(8,128)(2,1)S(1)}, bf16[2,2,1,8,3584]{4,3,2,1,0:T(8,128)(2,1)}, u32[]{:S(2)}) copy-start(bf16[2,2,1,8,3584]{4,3,2,1,0:T(8,128)(2,1)} %param.10) | copy-start | bytes 688132
  261.0 193.1 %copy-start.13 = (bf16[2,1,8,3584]{3,2,1,0:T(8,128)(2,1)S(1)}, bf16[2,1,8,3584]{3,2,1,0:T(8,128)(2,1)}, u32[]{:S(2)}) copy-start(bf16[2,1,8,3584]{3,2,1,0:T(8,128)(2,1)} %param.8) | copy-start | bytes 344068
  261.0 194.5 %copy-start.14 = (bf16[2,1,8,3584]{3,2,1,0:T(8,128)(2,1)S(1)}, bf16[2,1,8,3584]{3,2,1,0:T(8,128)(2,1)}, u32[]{:S(2)}) copy-start(bf16[2,1,8,3584]{3,2,1,0:T(8,128)(2,1)} %param.11) | copy-start | bytes 344068
  456.6 127.4 %slice-start.4 = ((s8[8257536]{0:T(1024)(128)(4,1)}), s8[4194304]{0:T(1024)(128)(4,1)S(1)}, s32[]{:S(2)}) async-start(s8[8257536]{0:T(1024)(128)(4,1)} %bitcast.226), calls=%async_computation.12 | async-start | bytes 8388608
  457.4 90.0 %collective-permute-start = (bf16[2,8,3584]{2,1,0:T(8,128)(2,1)S(1)}, bf16[2,8,3584]{2,1,0:T(8,128)(2,1)S(1)}, u32[]{:S(2)}, u32[]{:S(2)}) collective-permute-start(bf16[2,8,3584]{2,1,0:T(8,128)(2,1)S(1)} %get-tuple-element.51), channel_id=1, source_target_pairs={{0,16},{16,32},{32,48},{48,64},{64,80},{80,96},{96,112},{1,17},{17... | collective-permute-start | bytes 344072 | tf_op jit(solution)/shard_map/ppermute | solution.py:20
  461.5 85.9 %collective-permute-start.1 = (bf16[2,8,3584]{2,1,0:T(8,128)(2,1)S(1)}, bf16[2,8,3584]{2,1,0:T(8,128)(2,1)S(1)}, u32[]{:S(2)}, u32[]{:S(2)}) collective-permute-start(bf16[2,8,3584]{2,1,0:T(8,128)(2,1)S(1)} %get-tuple-element.49), channel_id=1, source_target_pairs={{16,0},{32,16},{48,32},{64,48},{80,64},{96,80},{112,96},{17,1},{33... | collective-permute-start | bytes 344072 | tf_op jit(solution)/shard_map/ppermute | solution.py:20
  508.1 39.3 %copy-start.17 = (bf16[1,2,8,3584]{3,2,1,0:T(8,128)(2,1)S(1)}, bf16[1,2,8,3584]{3,2,1,0:T(8,128)(2,1)}, u32[]{:S(2)}) copy-start(bf16[1,2,8,3584]{3,2,1,0:T(8,128)(2,1)} %param.12) | copy-start | bytes 344068
  508.1 75.9 %slice-start.5 = ((s8[8257536]{0:T(1024)(128)(4,1)}), s8[4063232]{0:T(1024)(128)(4,1)S(1)}, s32[]{:S(2)}) async-start(s8[8257536]{0:T(1024)(128)(4,1)} %bitcast.226), calls=%async_computation.13 | async-start | bytes 8126464
  542.8 40.2 %copy-start.2 = (bf16[128,3584]{1,0:T(8,128)(2,1)}, bf16[128,3584]{1,0:T(8,128)(2,1)S(1)}, u32[]{:S(2)}) copy-start(bf16[128,3584]{1,0:T(8,128)(2,1)S(1)} %all_gather.45) | copy-start | bytes 2752516
  542.8 45.7 %slice-start.2 = ((s8[8257536]{0:T(1024)(128)(4,1)}), s8[4194304]{0:T(1024)(128)(4,1)S(1)}, s32[]{:S(2)}) async-start(s8[8257536]{0:T(1024)(128)(4,1)} %bitcast.220), calls=%async_computation.10 | async-start | bytes 8388608
  547.4 37.8 %copy-start.19 = (bf16[2,8,3584]{2,1,0:T(8,128)(2,1)}, bf16[2,8,3584]{2,1,0:T(8,128)(2,1)S(1)}, u32[]{:S(2)}) copy-start(bf16[2,8,3584]{2,1,0:T(8,128)(2,1)S(1)} %collective-permute-done) | copy-start | bytes 344068
  547.4 37.8 %copy-start.20 = (bf16[2,8,3584]{2,1,0:T(8,128)(2,1)}, bf16[2,8,3584]{2,1,0:T(8,128)(2,1)S(1)}, u32[]{:S(2)}) copy-start(bf16[2,8,3584]{2,1,0:T(8,128)(2,1)S(1)} %collective-permute-done.1) | copy-start | bytes 344068
  583.0 2.3 copy-start.8
  584.0 4.5 slice-start.3
  624.9 31.1 %copy-start.18 = (bf16[1,2,8,3584]{3,2,1,0:T(8,128)(2,1)S(1)}, bf16[1,2,8,3584]{3,2,1,0:T(8,128)(2,1)}, u32[]{:S(2)}) copy-start(bf16[1,2,8,3584]{3,2,1,0:T(8,128)(2,1)} %param.9) | copy-start | bytes 344068
  624.9 139.2 %all-to-all-start = ((bf16[8,72,3584]{2,1,0:T(8,128)(2,1)}), bf16[8,72,3584]{2,1,0:T(8,128)(2,1)}, u32[]{:S(2)}, u32[]{:S(2)}) async-start(bf16[8,72,3584]{2,1,0:T(8,128)(2,1)} %bitcast.222), calls=%async_computation.2 | async-start | bytes 8257536 | tf_op jit(solution)/shard_map/all_to_all | solution.py:69
  656.1 286.4 %reduce-scatter.5.cloned.1.call-start = ((), (), s32[]{:S(2)}) async-start(), calls=%async_computation.7 | async-start | bytes 7798784 | tf_op jit(solution)/shard_map/reduce_scatter | solution.py:136
  751.9 3.2 copy-start.11
  752.0 3.3 copy-start.12
  764.1 65.4 %all-to-all-start.2 = ((bf16[8,72,3584]{2,1,0:T(8,128)(2,1)}), bf16[8,72,3584]{2,1,0:T(8,128)(2,1)}, u32[]{:S(2)}, u32[]{:S(2)}) async-start(bf16[8,72,3584]{2,1,0:T(8,128)(2,1)} %bitcast.223), calls=%async_computation.4 | async-start | bytes 8257536 | tf_op jit(solution)/shard_map/all_to_all | solution.py:69
  829.5 53.5 %all-to-all-start.1 = ((bf16[8,72,3584]{2,1,0:T(8,128)(2,1)}), bf16[8,72,3584]{2,1,0:T(8,128)(2,1)}, u32[]{:S(2)}, u32[]{:S(2)}) async-start(bf16[8,72,3584]{2,1,0:T(8,128)(2,1)} %rev.7), calls=%async_computation.3 | async-start | bytes 8257536 | tf_op jit(solution)/shard_map/all_to_all | solution.py:69
  839.2 49.1 %copy-start.1 = (bf16[128,3584]{1,0:T(8,128)(2,1)S(1)}, bf16[128,3584]{1,0:T(8,128)(2,1)}, u32[]{:S(2)}) copy-start(bf16[128,3584]{1,0:T(8,128)(2,1)} %copy-done) | copy-start | bytes 2752516
  839.2 49.1 %copy-start.3 = (bf16[128,3584]{1,0:T(8,128)(2,1)S(1)}, bf16[128,3584]{1,0:T(8,128)(2,1)}, u32[]{:S(2)}) copy-start(bf16[128,3584]{1,0:T(8,128)(2,1)} %copy-done.2) | copy-start | bytes 2752516
  883.1 53.5 %all-to-all-start.3 = ((bf16[8,72,3584]{2,1,0:T(8,128)(2,1)}), bf16[8,72,3584]{2,1,0:T(8,128)(2,1)}, u32[]{:S(2)}, u32[]{:S(2)}) async-start(bf16[8,72,3584]{2,1,0:T(8,128)(2,1)} %rev.8), calls=%async_computation.5 | async-start | bytes 8257536 | tf_op jit(solution)/shard_map/all_to_all | solution.py:69
  936.6 8.3 copy-start.16
  936.6 9.1 copy-start.15
  (4 other events, 5.8 us)
Sparse Core Ops, SparseCore 0:
  261.2 192.9 reduce-scatter.2
  758.6 164.6 reduce-scatter.4
where the time goes:
time: 954 us; the launch traced here: 953 us
  blocking collectives  435 us (46%)
  waiting for transfers between devices  324 us (34%)
  matrix products  81.8 us (9%)
  starting transfers between devices  65 us (7%)
  other arithmetic  20.5 us (2%)
  between operations  14.4 us (2%)
  local copies, waits for them, and re-layouts  13.3 us (1%)
    reduce_scatter x2, waiting for transfers between devices, body(): lax.psum_scatter(combine(), ('dp', 'tensor'), scatter_dimension=0, tiled=...  193 us
    all_to_all x4, waiting for transfers between devices, mirror_finished(): lax.all_to_all(for_sending(blocks), 'section', split_axis=0, concat_axis=...  130 us
    all_gather x2, blocking collectives, body(): lax.all_gather(trailing[1][2], ('dp', 'tensor'), axis=0, tiled=True)  80.5 us
    all_gather x2, blocking collectives, body(): lax.all_gather(leading[0][2], ('dp', 'tensor'), axis=0, tiled=True)  73.7 us
    all_gather x2, blocking collectives, body(): lax.all_gather(leading[1][2], ('dp', 'tensor'), axis=0, tiled=True)  71.8 us
    all_gather x2, blocking collectives, body(): lax.all_gather(upstream[0], ('dp', 'tensor'), axis=0, tiled=True)  70.8 us
    all_gather x2, blocking collectives, body(): lax.all_gather(upstream[1], ('dp', 'tensor'), axis=0, tiled=True)  70 us
    all_gather x2, blocking collectives, body(): lax.all_gather(trailing[0][2], ('dp', 'tensor'), axis=0, tiled=True)  68 us
  transfers between devices with their start and end apart: 8, of which 4 were waited for; matrix products, arithmetic and copies ran while one was open for 6% of the time, Pallas kernels for 0%

commit v1 on v0

v1 whole, which is shorter than its diff:
```python
import jax
import jax.numpy as jnp
from jax import lax
from jax.sharding import PartitionSpec as P

EPSILON = 1e-06
GROUP = ("dp", "tensor")


def contract_last(former, latter):
    return lax.dot_general(
        former, latter, (((1,), (1,)), ((), ())), preferred_element_type=jnp.float32
    )


def contract_first(former, latter):
    return lax.dot_general(
        former, latter, (((0,), (0,)), ((), ())), preferred_element_type=jnp.float32
    )


def normalize(states, scaling):
    widened = states.astype(jnp.float32)
    factor = lax.rsqrt(jnp.mean(widened * widened, axis=-1, keepdims=True) + EPSILON)
    return widened, factor, (widened * factor * scaling).astype(jnp.bfloat16)


def norm_back(widened, factor, scaling, upstream, d_normed):
    scaled = d_normed * scaling
    unit_rows = widened * factor
    d_norm = factor * (scaled - unit_rows * jnp.mean(unit_rows * scaled, axis=-1, keepdims=True))
    return (upstream.astype(jnp.float32) + d_norm).astype(jnp.bfloat16)


def gather(block):
    return lax.all_gather(block, GROUP, axis=0, tiled=True)


def spread_sum(partial):
    count = lax.axis_size(GROUP)
    blocks = partial.astype(jnp.bfloat16)
    blocks = lax.all_to_all(blocks, GROUP, split_axis=0, concat_axis=0, tiled=True)
    return blocks.reshape((count, -1) + partial.shape[1:]).astype(jnp.float32).sum(0)


def body(states_in, entering, saved, cotangent, cot_entering, gains, up_rows, down_rows):
    sections = lax.axis_size("section")
    position = lax.axis_index("section")
    mirror = [(i, sections - 1 - i) for i in range(sections)]
    gain = lax.dynamic_index_in_dim(gains, position, 0, keepdims=True).astype(jnp.float32)
    up, down = up_rows[0, 0], down_rows[0, 0]
    periods = saved.shape[0]
    far = jnp.concatenate([states_in[1], cotangent[1]] + [saved[k, 1] for k in range(periods)], 0)
    far = lax.ppermute(far, "section", mirror)
    rows = jnp.concatenate([states_in[0, 0], far[0]], 0)
    grads = jnp.concatenate([cotangent[0, 0], far[1]], 0)
    stored = [jnp.concatenate([saved[k, 0, 0], far[2 + k]], 0) for k in range(periods)]
    produced_all, returned_all, terms = [], [], []
    for period in range(periods):
        wide, _, lead = normalize(rows, gain)
        wide_back, factor_back, trail = normalize(stored[period], gain)
        lead_all, trail_all, grads_all = gather(lead), gather(trail), gather(grads)
        acted = jax.nn.silu(contract_last(lead_all, up)).astype(jnp.bfloat16)
        hidden = contract_last(trail_all, up)
        gating = jax.nn.sigmoid(hidden)
        d_hidden = (
            contract_last(grads_all, down) * gating * (1.0 + hidden * (1.0 - gating))
        ).astype(jnp.bfloat16)
        acted_back = (hidden * gating).astype(jnp.bfloat16)
        terms.append((acted_back, grads_all, d_hidden, trail_all))
        out = jnp.dot(acted, down, preferred_element_type=jnp.float32)
        d_normed = jnp.dot(d_hidden, up, preferred_element_type=jnp.float32)
        produced = (wide + spread_sum(out)).astype(jnp.bfloat16)
        returned = norm_back(wide_back, factor_back, gain, grads, spread_sum(d_normed))
        produced_all.append(produced)
        returned_all.append(returned)
        if period + 1 < periods:
            onward = lax.ppermute(produced, "section", [(i, i + 1) for i in range(sections - 1)])
            back = lax.ppermute(returned, "section", [(i + 1, i) for i in range(sections - 1)])
            fresh = jnp.concatenate([entering[period, 0], entering[period, 1]], 0)
            fresh_back = jnp.concatenate([cot_entering[period, 0], cot_entering[period, 1]], 0)
            rows = jnp.where(position == 0, fresh, onward)
            grads = jnp.where(position == sections - 1, fresh_back, back)
    acted_back, grads_all, d_hidden, trail_all = (jnp.concatenate(m, 0) for m in zip(*terms))
    grad_up = contract_first(d_hidden, trail_all).astype(jnp.bfloat16)[None]
    grad_down = contract_first(acted_back, grads_all).astype(jnp.bfloat16)[None]
    half = produced_all[0].shape[0] // 2
    results = jnp.stack([jnp.stack(produced_all), jnp.stack(returned_all)])
    results_far = lax.ppermute(results[:, :, half:], "section", mirror)
    both = jnp.stack([results[:, :, :half], results_far], 2)[:, :, :, None]
    return both[0], both[1], grad_up, grad_down


def solution(mesh):
    group = ("dp", "tensor")
    placed = (
        P(None, "section", group, None),
        P(None, None, group, None),
        P(None, None, "section", group, None),
        P(None, "section", group, None),
        P(None, None, group, None),
        P(),
        P("section", None, group, None),
        P("section", None, group, None),
    )
    return jax.shard_map(
        body,
        mesh=mesh,
        in_specs=placed,
        out_specs=(
            P(None, None, "section", group, None),
            P(None, None, "section", group, None),
            P("section", group, None),
            P("section", group, None),
        ),
        check_vma=False,
    )
```

time: 954 us -> 628 us (0.66)
  blocking collectives: 435 us -> 0 us
  waiting for transfers between devices: 324 us -> 470 us
  matrix products: 81.8 us -> 59.6 us
  other arithmetic: 20.5 us -> 7.68 us
  local copies, waits for them, and re-layouts: 13.3 us -> 3.43 us
    all_gather x12 -> x0, blocking collectives: 435 us -> none  [the longest x2 80.5 us: body(): lax.all_gather(trailing[1][2], ('dp', 'tensor'), axis=0, tiled=True)]
    all_gather x0 -> x6, waiting for transfers between devices: none -> 403 us  [gather(): return lax.all_gather(block, GROUP, axis=0, tiled=True)]
    reduce_scatter x2 -> x0, waiting for transfers between devices: 193 us -> none  [body(): lax.psum_scatter(combine(), ('dp', 'tensor'), scatter_dimension=0, tiled=...]
    all_to_all x4, waiting for transfers between devices: 130 us -> 55.4 us  [spread_sum(): lax.all_to_all(blocks, GROUP, split_axis=0, concat_axis=0, tiled=True)]
    ppermute x2 -> x4, starting transfers between devices: 6 us -> 49.5 us  [the longest x1 15.8 us: body(): lax.ppermute(produced, 'section', [(i, i + 1) for i in range(sections - 1)])]
    all_to_all x4, starting transfers between devices: 58.9 us -> 21.9 us  [spread_sum(): lax.all_to_all(blocks, GROUP, split_axis=0, concat_axis=0, tiled=True)]
    ppermute x2 -> x4, waiting for transfers between devices: 0.01 us -> 10.9 us  [the longest x1 4.85 us: body(): far = lax.ppermute(far, 'section', mirror)]
    dot_general x8 -> x4, matrix products: 40.7 us -> 30.4 us  [the longest x2 20.3 us: body(): out = jnp.dot(acted, down, preferred_element_type=jnp.float32)]
  transfers between devices with their start and end apart: 8 -> 14, of which waited for: 4 -> 14; matrix products, arithmetic and copies ran while one was open for 6% -> 4% of each run, Pallas kernels for 0% -> 0%
where the time goes in v1:
time: 628 us; the launch traced here: 627 us
  waiting for transfers between devices  470 us (75%)
  starting transfers between devices  71.6 us (11%)
  matrix products  59.6 us (9%)
  between operations  14.3 us (2%)
  other arithmetic  7.68 us (1%)
    all_gather x6, waiting for transfers between devices, gather(): return lax.all_gather(block, GROUP, axis=0, tiled=True)  403 us
    all_to_all x4, waiting for transfers between devices, spread_sum(): lax.all_to_all(blocks, GROUP, split_axis=0, concat_axis=0, tiled=True)  55.4 us
    all_to_all x4, starting transfers between devices, spread_sum(): lax.all_to_all(blocks, GROUP, split_axis=0, concat_axis=0, tiled=True)  21.9 us
    dot_general x2, matrix products, body(): out = jnp.dot(acted, down, preferred_element_type=jnp.float32)  20.3 us
    dot_general x4, matrix products, contract_last(): lax.dot_general(former, latter, (((1,), (1,)), ((), ())), preferred_eleme...  17.4 us
    ppermute x1, starting transfers between devices, body(): lax.ppermute(produced, 'section', [(i, i + 1) for i in range(sections - 1)])  15.8 us
    ppermute x1, starting transfers between devices, body(): results_far = lax.ppermute(results[:, :, half:], 'section', mirror)  15.1 us
    ppermute x1, starting transfers between devices, body(): lax.ppermute(returned, 'section', [(i + 1, i) for i in range(sections - 1)])  14.4 us
  transfers between devices with their start and end apart: 14, of which 14 were waited for; matrix products, arithmetic and copies ran while one was open for 4% of the time, Pallas kernels for 0%

profile of v1, /device:TPU:1, one launch (start us, length us, event | category | flops | bytes accessed | tf_op | source)
XLA Modules:
  0.0 627.2 jit_solution(10703472062257628969)
XLA Ops:
  8.9 0.9 slice_bitcast_fusion.10
  9.9 4.2 collective-permute-start
  15.0 4.9 collective-permute-done
  21.7 67.7 %all-gather.13.cloned.1.call-done = bf16[256,3584]{1,0:T(8,128)(2,1)} async-done(((bf16[16,3584]{1,0:T(8,128)(2,1)}), bf16[256,3584]{1,0:T(8,128)(2,1)}) %all-gather.13.cloned.1.call-update) | async-done | bytes 1835024 | tf_op jit(solution)/shard_map/all_gather | solution.py:36
  89.3 4.7 multiply_convert_fusion.1
  94.0 74.1 %all-gather.11.cloned.1.call-done = bf16[256,3584]{1,0:T(8,128)(2,1)} async-done(((bf16[16,3584]{1,0:T(8,128)(2,1)}), bf16[256,3584]{1,0:T(8,128)(2,1)}) %all-gather.11.cloned.1.call-update) | async-done | bytes 1835024 | tf_op jit(solution)/shard_map/all_gather | solution.py:36
  168.1 4.0 fusion.46
  172.8 5.0 convolution_convert_fusion.3
  177.8 5.5 all-to-all-start.2
  184.2 15.0 %all-to-all-done.2 = bf16[16,16,3584]{2,1,0:T(8,128)(2,1)S(1)} async-done(((bf16[16,16,3584]{2,1,0:T(8,128)(2,1)}), bf16[16,16,3584]{2,1,0:T(8,128)(2,1)S(1)}, u32[]{:S(2)}, u32[]{:S(2)}) %all-to-all-start.2) | async-done | bytes 1835040 | tf_op jit(solution)/shard_map/all_to_all | solution.py:42
  199.8 14.4 %collective-permute-start.2 = (bf16[16,3584]{1,0:T(8,128)(2,1)S(1)}, bf16[16,3584]{1,0:T(8,128)(2,1)S(1)}, u32[]{:S(2)}, u32[]{:S(2)}) collective-permute-start(bf16[16,3584]{1,0:T(8,128)(2,1)S(1)} %fusion.79), channel_id=1, source_target_pairs={{16,0},{32,16},{48,32},{64,48},{80,64},{96,80},{112,96},{17,1},{33... | collective-permute-start | bytes 344072 | tf_op jit(solution)/shard_map/ppermute | solution.py:79
  214.2 3.7 collective-permute-done.2
  218.6 45.4 %all-gather.17.cloned.1.call-done = bf16[256,3584]{1,0:T(8,128)(2,1)} async-done(((bf16[16,3584]{1,0:T(8,128)(2,1)}), bf16[256,3584]{1,0:T(8,128)(2,1)}) %all-gather.17.cloned.1.call-update) | async-done | bytes 1835024 | tf_op jit(solution)/shard_map/all_gather | solution.py:36
  264.0 4.7 multiply_convert_fusion
  268.8 74.7 %all-gather.15.cloned.1.call-done = bf16[256,3584]{1,0:T(8,128)(2,1)} async-done(((bf16[16,3584]{1,0:T(8,128)(2,1)}), bf16[256,3584]{1,0:T(8,128)(2,1)}) %all-gather.15.cloned.1.call-update) | async-done | bytes 1835024 | tf_op jit(solution)/shard_map/all_gather | solution.py:36
  343.4 4.0 fusion.49
  347.4 5.1 convolution_convert_fusion.2
  352.5 5.4 all-to-all-start.3
  358.2 15.6 %all-to-all-done.3 = bf16[16,16,3584]{2,1,0:T(8,128)(2,1)S(1)} async-done(((bf16[16,16,3584]{2,1,0:T(8,128)(2,1)}), bf16[16,16,3584]{2,1,0:T(8,128)(2,1)S(1)}, u32[]{:S(2)}, u32[]{:S(2)}) %all-to-all-start.3) | async-done | bytes 1835040 | tf_op jit(solution)/shard_map/all_to_all | solution.py:42
  374.9 76.5 %all-gather.7.cloned.1.call-done = bf16[256,3584]{1,0:T(8,128)(2,1)} async-done(((bf16[16,3584]{1,0:T(8,128)(2,1)}), bf16[256,3584]{1,0:T(8,128)(2,1)}) %all-gather.7.cloned.1.call-update) | async-done | bytes 1835024 | tf_op jit(solution)/shard_map/all_gather | solution.py:36
  451.4 10.1 %convolution_convert_fusion.5 = bf16[256,3584]{1,0:T(8,128)(2,1)} fusion(bf16[1,2,576,3584]{3,2,1,0:T(8,128)(2,1)} %param.15, bf16[256,3584]{1,0:T(8,128)(2,1)} %all-gather.7.cloned.1.call-done, bf16[1,2,576,3584]{3,2,1,0:T(8,128)(2,1)} %param.14), kind=kOutput, calls=%fused_computation.7 | convolution fusion | flops 2115584000 | bytes 11927552 | tf_op jit(solution)/shard_map/dot_general | solution.py:71
  461.5 5.6 all-to-all-start
  467.2 15.7 %all-to-all-done = bf16[16,16,3584]{2,1,0:T(8,128)(2,1)S(1)} async-done(((bf16[16,16,3584]{2,1,0:T(8,128)(2,1)}), bf16[16,16,3584]{2,1,0:T(8,128)(2,1)S(1)}, u32[]{:S(2)}, u32[]{:S(2)}) %all-to-all-start) | async-done | bytes 1835040 | tf_op jit(solution)/shard_map/all_to_all | solution.py:42
  483.2 15.8 %collective-permute-start.1 = (bf16[16,3584]{1,0:T(8,128)(2,1)S(1)}, bf16[16,3584]{1,0:T(8,128)(2,1)S(1)}, u32[]{:S(2)}, u32[]{:S(2)}) collective-permute-start(bf16[16,3584]{1,0:T(8,128)(2,1)S(1)} %fusion.91), channel_id=1, source_target_pairs={{0,16},{16,32},{32,48},{48,64},{64,80},{80,96},{96,112},{1,17},{17... | collective-permute-start | bytes 344072 | tf_op jit(solution)/shard_map/ppermute | solution.py:78
  499.0 1.6 collective-permute-done.1
  501.6 65.2 %all-gather.9.cloned.1.call-done = bf16[256,3584]{1,0:T(8,128)(2,1)} async-done(((bf16[16,3584]{1,0:T(8,128)(2,1)}), bf16[256,3584]{1,0:T(8,128)(2,1)}) %all-gather.9.cloned.1.call-update) | async-done | bytes 1835024 | tf_op jit(solution)/shard_map/all_gather | solution.py:36
  566.7 10.1 %convolution_convert_fusion.4 = bf16[256,3584]{1,0:T(8,128)(2,1)} fusion(bf16[1,2,576,3584]{3,2,1,0:T(8,128)(2,1)} %param.15, bf16[256,3584]{1,0:T(8,128)(2,1)} %all-gather.9.cloned.1.call-done, bf16[1,2,576,3584]{3,2,1,0:T(8,128)(2,1)} %param.14), kind=kOutput, calls=%fused_computation.6 | convolution fusion | flops 2115584000 | bytes 11927552 | tf_op jit(solution)/shard_map/dot_general | solution.py:71
  576.9 5.4 all-to-all-start.1
  582.4 6.5 %fusion = bf16[1,576,3584]{2,1,0:T(8,128)(2,1)} fusion(bf16[256,3584]{1,0:T(8,128)(2,1)} %all-gather.17.cloned.1.call-done, bf16[256,3584]{1,0:T(8,128)(2,1)} %all-gather.13.cloned.1.call-done, bf16[256,576]{0,1:T(8,128)(2,1)} %copy-done.6, bf16[256,576]{0,1:T(8,128)(2,1)} %copy-done.5), kind=kOutput, calls=%fused_computation.2 | convolution fusion | flops 2124513280 | bytes 8388608 | tf_op jit(solution)/shard_map/dot_general | solution.py:17
  589.0 9.1 %all-to-all-done.1 = bf16[16,16,3584]{2,1,0:T(8,128)(2,1)S(1)} async-done(((bf16[16,16,3584]{2,1,0:T(8,128)(2,1)}), bf16[16,16,3584]{2,1,0:T(8,128)(2,1)S(1)}, u32[]{:S(2)}, u32[]{:S(2)}) %all-to-all-start.1) | async-done | bytes 1835040 | tf_op jit(solution)/shard_map/all_to_all | solution.py:42
  598.4 15.1 %collective-permute-start.3 = (bf16[2,2,8,3584]{3,2,1,0:T(8,128)(2,1)S(1)}, bf16[2,2,8,3584]{3,2,1,0:T(8,128)(2,1)S(1)}, u32[]{:S(2)}, u32[]{:S(2)}) collective-permute-start(bf16[2,2,8,3584]{3,2,1,0:T(8,128)(2,1)S(1)} %get-tuple-element.8), channel_id=1, source_target_pairs={{0,112},{16,96},{32,80},{48,64},{64,48},{80,32},{96,16},{112,0},{1... | collective-permute-start | bytes 688136 | tf_op jit(solution)/shard_map/ppermute | solution.py:89
  613.5 5.3 fusion.1
  (64 shorter events, 11.9 us)
Async XLA Ops:
  7.2 82.1 %all-gather.13.cloned.1.call-start = ((), (), s32[]{:S(2)}) async-start(), calls=%async_computation.7 | async-start | bytes 1949696 | tf_op jit(solution)/shard_map/all_gather | solution.py:36
  9.9 9.9 %collective-permute-start = (bf16[4,8,3584]{2,1,0:T(8,128)(2,1)S(1)}, bf16[4,8,3584]{2,1,0:T(8,128)(2,1)S(1)}, u32[]{:S(2)}, u32[]{:S(2)}) collective-permute-start(bf16[4,8,3584]{2,1,0:T(8,128)(2,1)S(1)} %pad_maximum_fusion.2), channel_id=1, source_target_pairs={{0,112},{16,96},{32,80},{48,64},{64,48},{80,32},{96,16},{112,0},{1... | collective-permute-start | bytes 688136 | tf_op jit(solution)/shard_map/ppermute | solution.py:54
  20.9 147.2 %all-gather.11.cloned.1.call-start = ((), (), s32[]{:S(2)}) async-start(), calls=%async_computation.6 | async-start | bytes 1949696 | tf_op jit(solution)/shard_map/all_gather | solution.py:36
  172.1 0.7 copy-start.5
  177.8 36.4 %copy-start.1 = (bf16[1,2,8,3584]{3,2,1,0:T(8,128)(2,1)S(1)}, bf16[1,2,8,3584]{3,2,1,0:T(8,128)(2,1)}, u32[]{:S(2)}) copy-start(bf16[1,2,8,3584]{3,2,1,0:T(8,128)(2,1)} %param.12) | copy-start | bytes 344068
  177.8 21.4 %all-to-all-start.2 = ((bf16[16,16,3584]{2,1,0:T(8,128)(2,1)}), bf16[16,16,3584]{2,1,0:T(8,128)(2,1)S(1)}, u32[]{:S(2)}, u32[]{:S(2)}) async-start(bf16[16,16,3584]{2,1,0:T(8,128)(2,1)} %bitcast.132), calls=%async_computation.2 | async-start | bytes 3670016 | tf_op jit(solution)/shard_map/all_to_all | solution.py:42
  183.4 80.7 %all-gather.17.cloned.1.call-start = ((), (), s32[]{:S(2)}) async-start(), calls=%async_computation.9 | async-start | bytes 1949696 | tf_op jit(solution)/shard_map/all_gather | solution.py:36
  184.1 159.3 %all-gather.15.cloned.1.call-start = ((), (), s32[]{:S(2)}) async-start(), calls=%async_computation.8 | async-start | bytes 1949696 | tf_op jit(solution)/shard_map/all_gather | solution.py:36
  199.8 18.1 %collective-permute-start.2 = (bf16[16,3584]{1,0:T(8,128)(2,1)S(1)}, bf16[16,3584]{1,0:T(8,128)(2,1)S(1)}, u32[]{:S(2)}, u32[]{:S(2)}) collective-permute-start(bf16[16,3584]{1,0:T(8,128)(2,1)S(1)} %fusion.79), channel_id=1, source_target_pairs={{16,0},{32,16},{48,32},{64,48},{80,64},{96,80},{112,96},{17,1},{33... | collective-permute-start | bytes 344072 | tf_op jit(solution)/shard_map/ppermute | solution.py:79
  347.4 5.1 copy-start.6
  352.5 21.2 %all-to-all-start.3 = ((bf16[16,16,3584]{2,1,0:T(8,128)(2,1)}), bf16[16,16,3584]{2,1,0:T(8,128)(2,1)S(1)}, u32[]{:S(2)}, u32[]{:S(2)}) async-start(bf16[16,16,3584]{2,1,0:T(8,128)(2,1)} %bitcast.134), calls=%async_computation.3 | async-start | bytes 3670016 | tf_op jit(solution)/shard_map/all_to_all | solution.py:42
  358.0 93.4 %all-gather.7.cloned.1.call-start = ((), (), s32[]{:S(2)}) async-start(), calls=%async_computation.4 | async-start | bytes 1949696 | tf_op jit(solution)/shard_map/all_gather | solution.py:36
  461.5 5.6 copy-start.2
  461.5 39.2 %copy-start = (bf16[16,3584]{1,0:T(8,128)(2,1)S(1)}, bf16[16,3584]{1,0:T(8,128)(2,1)}, u32[]{:S(2)}) copy-start(bf16[16,3584]{1,0:T(8,128)(2,1)} %maximum_select_fusion.1) | copy-start | bytes 344068
  461.5 21.4 %all-to-all-start = ((bf16[16,16,3584]{2,1,0:T(8,128)(2,1)}), bf16[16,16,3584]{2,1,0:T(8,128)(2,1)S(1)}, u32[]{:S(2)}, u32[]{:S(2)}) async-start(bf16[16,16,3584]{2,1,0:T(8,128)(2,1)} %bitcast.133), calls=%async_computation | async-start | bytes 3670016 | tf_op jit(solution)/shard_map/all_to_all | solution.py:42
  467.1 99.6 %all-gather.9.cloned.1.call-start = ((), (), s32[]{:S(2)}) async-start(), calls=%async_computation.5 | async-start | bytes 1949696 | tf_op jit(solution)/shard_map/all_gather | solution.py:36
  483.2 17.4 %collective-permute-start.1 = (bf16[16,3584]{1,0:T(8,128)(2,1)S(1)}, bf16[16,3584]{1,0:T(8,128)(2,1)S(1)}, u32[]{:S(2)}, u32[]{:S(2)}) collective-permute-start(bf16[16,3584]{1,0:T(8,128)(2,1)S(1)} %fusion.91), channel_id=1, source_target_pairs={{0,16},{16,32},{32,48},{48,64},{64,80},{80,96},{96,112},{1,17},{17... | collective-permute-start | bytes 344072 | tf_op jit(solution)/shard_map/ppermute | solution.py:78
  576.9 21.2 %all-to-all-start.1 = ((bf16[16,16,3584]{2,1,0:T(8,128)(2,1)}), bf16[16,16,3584]{2,1,0:T(8,128)(2,1)S(1)}, u32[]{:S(2)}, u32[]{:S(2)}) async-start(bf16[16,16,3584]{2,1,0:T(8,128)(2,1)} %bitcast.131), calls=%async_computation.1 | async-start | bytes 3670016 | tf_op jit(solution)/shard_map/all_to_all | solution.py:42
  589.0 24.5 %copy-start.7 = (bf16[256,576]{0,1:T(8,128)(2,1)S(1)}, bf16[256,576]{0,1:T(8,128)(2,1)}, u32[]{:S(2)}) copy-start(bf16[256,576]{0,1:T(8,128)(2,1)} %get-tuple-element.40) | copy-start | bytes 884740
  598.1 15.4 %copy-start.3 = (bf16[256,3584]{1,0:T(8,128)(2,1)S(1)}, bf16[256,3584]{1,0:T(8,128)(2,1)}, u32[]{:S(2)}) copy-start(bf16[256,3584]{1,0:T(8,128)(2,1)} %all-gather.11.cloned.1.call-done) | copy-start | bytes 5505028
  598.1 15.4 %copy-start.4 = (bf16[256,3584]{1,0:T(8,128)(2,1)S(1)}, bf16[256,3584]{1,0:T(8,128)(2,1)}, u32[]{:S(2)}) copy-start(bf16[256,3584]{1,0:T(8,128)(2,1)} %all-gather.15.cloned.1.call-done) | copy-start | bytes 5505028
  598.4 21.1 %collective-permute-start.3 = (bf16[2,2,8,3584]{3,2,1,0:T(8,128)(2,1)S(1)}, bf16[2,2,8,3584]{3,2,1,0:T(8,128)(2,1)S(1)}, u32[]{:S(2)}, u32[]{:S(2)}) collective-permute-start(bf16[2,2,8,3584]{3,2,1,0:T(8,128)(2,1)S(1)} %get-tuple-element.8), channel_id=1, source_target_pairs={{0,112},{16,96},{32,80},{48,64},{64,48},{80,32},{96,16},{112,0},{1... | collective-permute-start | bytes 688136 | tf_op jit(solution)/shard_map/ppermute | solution.py:89
Sparse Core Ops, SparseCore 0:
  21.0 68.2 all-gather.12
  91.5 76.5 all-gather.10
  186.4 77.5 all-gather.16
  266.1 77.2 all-gather.14
  375.0 76.3 all-gather.6
  501.7 64.9 all-gather.8

commit v2 on v1

v2 whole, which is shorter than its diff:
```python
import functools

import jax
import jax.numpy as jnp
from jax import lax
from jax.experimental import pallas as pl
from jax.experimental.pallas import tpu as pltpu
from jax.sharding import PartitionSpec as P

EPSILON = 1e-06
MESH = pl.DeviceIdType.MESH
F32, BF16 = jnp.float32, jnp.bfloat16
FA, NA, GA, NB, FB, GB = range(6)
RING = 4


def contract_last(former, latter):
    return lax.dot_general(former, latter, (((1,), (1,)), ((), ())), preferred_element_type=F32)


def mean(value):
    return jnp.mean(value, axis=-1, keepdims=True)


def kernel(
    states_in, entering, saved, cotangent, cot_entering, gains, up_rows, down_rows,
    states_out, input_grads, grad_up, grad_down,
    up, down, gathered, partial, pass_on, from_prev, from_next, summed, scattered,
    rows, grads, far_out, far_in, hop_out, hop_in, mirror_out, mirror_in,
    slopes, hidden_kept, active_kept, flipped, staged,
    load_sem, store_sem, ag_send, ag_recv, rs_send, rs_recv, far_send, far_recv,
    hop_send, hop_recv, mirror_send, mirror_recv,
):
    s = lax.axis_index("section")
    d = lax.axis_index("dp")
    t = lax.axis_index("tensor")
    sections = lax.axis_size("section")
    width = up.shape[-1]
    half = width // 2
    features = 2 * width
    units = up.shape[1]
    place = {"x": d % RING, "z": (d // RING) * 2 + t}

    def device(section, x, z):
        return (section, (z // 2) * RING + x, z % 2)

    def along(axis, step):
        moved = dict(place)
        moved[axis] = (place[axis] + step) % RING
        return device(s, moved["x"], moved["z"])

    mirror = device(sections - 1 - s, place["x"], place["z"])
    after = device((s + 1) % sections, place["x"], place["z"])
    before = device((s + sections - 1) % sections, place["x"], place["z"])

    loads = [
        pltpu.make_async_copy(
            source.at[0, 0, :, pl.ds(h * width, width)], target.at[h], load_sem.at[2 * n + h]
        )
        for n, (source, target) in enumerate(((up_rows, up), (down_rows, down)))
        for h in range(2)
    ]
    for load in loads:
        load.start()

    barrier = pltpu.get_barrier_semaphore()
    partners = [along(axis, step) for axis in "xz" for step in (1, 2, 3)] + [mirror, after, before]
    for partner in partners:
        pl.semaphore_signal(barrier, inc=1, device_id=partner, device_id_type=MESH)
    pl.semaphore_wait(barrier, len(partners))

    sends = []

    def send(source, target, send_sem, recv_sem, device_id):
        copy = pltpu.make_async_remote_copy(
            src_ref=source, dst_ref=target, send_sem=send_sem, recv_sem=recv_sem,
            device_id=device_id, device_id_type=MESH,
        )
        copy.start()
        sends.append(copy)

    def arrive(target, send_sem, recv_sem, device_id):
        pltpu.make_async_remote_copy(
            src_ref=target, dst_ref=target, send_sem=send_sem, recv_sem=recv_sem,
            device_id=device_id, device_id_type=MESH,
        ).wait_recv()

    inner, outer = ("x", "z"), ("z", "x")
    low, high, whole = pl.ds(0, half), pl.ds(half, half), pl.ds(0, width)

    def slab(ref, index, h, step, lanes):
        at = (place[outer[h]] + step) % RING
        return ref.at[index, h, at, :, :, lanes] if h == 0 else ref.at[index, h, :, at, :, lanes]

    def block(ref, index, h, step):
        at = dict(place)
        at[inner[h]] = (place[inner[h]] + step) % RING
        return ref.at[index, h, at["z"], at["x"]]

    def gather_inner(a):
        for h in range(2):
            for step in (1, 3, 2):
                own = block(gathered, a, h, 0)
                sems = (ag_send.at[a, h, step - 1], ag_recv.at[a, h, step - 1])
                send(own, own, *sems, along(inner[h], step))

    def gather_outer(a):
        for h in range(2):
            for step in (1, 2, 3):
                sems = (ag_send.at[a, h, step - 1], ag_recv.at[a, h, step - 1])
                arrive(block(gathered, a, h, -step), *sems, along(inner[h], step))
            own = slab(gathered, a, h, 0, whole)
            for n, step in ((3, 1), (4, -1)):
                send(own, own, ag_send.at[a, h, n], ag_recv.at[a, h, n], along(outer[h], step))

    def gather_relay(a):
        for h in range(2):
            for n, step, lanes in ((3, 1, low), (4, -1, high)):
                sems = (ag_send.at[a, h, n], ag_recv.at[a, h, n])
                arrive(slab(gathered, a, h, -step, whole), *sems, along(outer[h], step))
                sems = (ag_send.at[a, h, n + 2], ag_recv.at[a, h, n + 2])
                passed = slab(gathered, a, h, -step, lanes)
                send(passed, passed, *sems, along(outer[h], step))

    def gather_end(a):
        for h in range(2):
            for n, step, lanes in ((5, 1, low), (6, -1, high)):
                sems = (ag_send.at[a, h, n], ag_recv.at[a, h, n])
                arrive(slab(gathered, a, h, -2 * step, lanes), *sems, along(outer[h], step))

    def scatter_start(p, h):
        def put(n, step, lanes, target, to):
            send(
                slab(partial, p, h, step, lanes), target.at[p, h, :, :, lanes],
                rs_send.at[p, h, n], rs_recv.at[p, h, n], along(outer[h], to),
            )

        put(0, 2, low, pass_on, 1)
        put(1, 2, high, pass_on, -1)
        put(2, 1, high, from_prev, 1)
        put(3, -1, low, from_next, -1)

    def scatter_relay(p):
        for h in range(2):
            for n, step, lanes, target in ((0, 1, low, from_prev), (1, -1, high, from_next)):
                passing = pass_on.at[p, h, :, :, lanes]
                arrive(passing, rs_send.at[p, h, n], rs_recv.at[p, h, n], along(outer[h], step))
                mine = slab(partial, p, h, step, lanes)
                mine[...] = (mine[...].astype(F32) + passing[...].astype(F32)).astype(BF16)
                send(
                    mine, target.at[p, h, :, :, lanes],
                    rs_send.at[p, h, n + 4], rs_recv.at[p, h, n + 4], along(outer[h], step),
                )

    def scatter_inner(p):
        for h in range(2):
            for n, lanes, target, step in (
                (2, high, from_prev, 1), (3, low, from_next, -1), (4, low, from_prev, 1), (5, high, from_next, -1),
            ):
                landed = target.at[p, h, :, :, lanes]
                arrive(landed, rs_send.at[p, h, n], rs_recv.at[p, h, n], along(outer[h], step))
            total = slab(partial, p, h, 0, whole)[...].astype(F32)
            total = total + from_prev[p, h].astype(F32) + from_next[p, h].astype(F32)
            summed[p, h] = total.astype(BF16)
            for step in (1, 3, 2):
                at = (place[inner[h]] + step) % RING
                send(
                    summed.at[p, h, at], scattered.at[p, h, step - 1],
                    rs_send.at[p, h, 5 + step], rs_recv.at[p, h, 5 + step], along(inner[h], step),
                )

    def scatter_end(p):
        halves = []
        for h in range(2):
            total = summed[p, h, pl.ds(place[inner[h]], 1)][0].astype(F32)
            for step in (1, 2, 3):
                landed = scattered.at[p, h, step - 1]
                sems = (rs_send.at[p, h, 5 + step], rs_recv.at[p, h, 5 + step])
                arrive(landed, *sems, along(inner[h], step))
                total = total + landed[...].astype(F32)
            halves.append(total)
        return jnp.concatenate(halves, axis=1)

    def put_block(a, value):
        value = value.astype(BF16)
        for h in range(2):
            block(gathered, a, h, 0)[...] = value[:, h * width : (h + 1) * width]

    def factor_of(value):
        return lax.rsqrt(mean(value * value) + EPSILON)

    def normed(value):
        return value * factor_of(value) * gain

    def tokens(a, h):
        return gathered[a, h].reshape(RING * RING * 16, width)

    def onto_units(a, weights):
        return contract_last(tokens(a, 0), weights[0]) + contract_last(tokens(a, 1), weights[1])

    def onto_features(p, value, weights):
        tile = 256
        for h in range(2):
            def one(n, carry):
                lanes = pl.ds(pl.multiple_of(n * tile, tile), tile)
                product = jnp.dot(value, weights[h, :, lanes], preferred_element_type=F32)
                partial[p, h, :, :, :, lanes] = product.astype(BF16).reshape(RING, RING, 16, tile)
                return carry

            lax.fori_loop(0, width // tile, one, 0)
            scatter_start(p, h)

    def forward(p, a):
        hidden = onto_units(a, up)
        active = (hidden * jax.nn.sigmoid(hidden)).astype(BF16)
        onto_features(p, active, down)

    def backward_hidden(period, a):
        hidden = onto_units(a, up)
        gating = jax.nn.sigmoid(hidden)
        active_kept[...] = (hidden * gating).astype(BF16)
        hidden_kept[...] = gating * (1.0 + hidden * (1.0 - gating))
        flipped[1, period] = active_kept[...].T

    def backward(p, period, a):
        slopes[...] = (onto_units(a, down) * hidden_kept[...]).astype(BF16)
        onto_features(p, slopes[...], up)

    def backward_keep(period):
        flipped[0, period] = slopes[...].T

    def weight_grad(kind, h, target, first, second):
        tile = 256

        def one(n, carry):
            lanes = pl.ds(pl.multiple_of(n * tile, tile), tile)
            total = jnp.dot(
                flipped[kind, 0], gathered[first, h, :, :, :, lanes].reshape(-1, tile), preferred_element_type=F32
            ) + jnp.dot(
                flipped[kind, 1], gathered[second, h, :, :, :, lanes].reshape(-1, tile), preferred_element_type=F32
            )
            staged[kind, h, :, lanes] = total.astype(BF16)
            return carry

        lax.fori_loop(0, width // tile, one, 0)
        copy = pltpu.make_async_copy(
            staged.at[kind, h], target.at[0, :, pl.ds(h * width, width)], store_sem.at[kind, h]
        )
        copy.start()
        return copy

    def hop(n, value, to):
        hop_out[n] = value.astype(BF16)
        send(hop_out.at[n], hop_in.at[n], hop_send.at[n], hop_recv.at[n], to)

    def hopped(n, to):
        arrive(hop_in.at[n], hop_send.at[n], hop_recv.at[n], to)
        return hop_in[n].astype(F32)

    def deliver(n, target, period, value):
        value = value.astype(BF16)
        mirror_out[n] = value
        send(mirror_out.at[n], mirror_in.at[n], mirror_send.at[n], mirror_recv.at[n], mirror)
        target[period, 0, 0] = value.astype(F32)[:8].astype(BF16)

    def delivered(n, target, period):
        arrive(mirror_in.at[n], mirror_send.at[n], mirror_recv.at[n], mirror)
        target[period, 1, 0] = mirror_in[n].astype(F32)[8:].astype(BF16)

    def wide(value):
        return value.astype(F32)

    def joined(first, second):
        return jnp.concatenate([wide(first), wide(second)], axis=0)

    far_out[0] = joined(states_in[1, 0], cotangent[1, 0]).astype(BF16)
    send(far_out.at[0], far_in.at[0], far_send.at[0], far_recv.at[0], mirror)
    far_out[1] = joined(saved[0, 1, 0], saved[1, 1, 0]).astype(BF16)
    send(far_out.at[1], far_in.at[1], far_send.at[1], far_recv.at[1], mirror)

    chosen = lax.broadcasted_iota(jnp.int32, gains.shape, 0) == s
    gain = jnp.sum(jnp.where(chosen, wide(gains[...]), 0.0), axis=0, keepdims=True)

    arrive(far_in.at[0], far_send.at[0], far_recv.at[0], mirror)
    far = wide(far_in[0])
    rows[0] = jnp.concatenate([wide(states_in[0, 0]), far[:8]], axis=0)
    put_block(FA, normed(rows[0]))
    gather_inner(FA)
    grads[0] = jnp.concatenate([wide(cotangent[0, 0]), far[8:]], axis=0)
    put_block(GA, grads[0])
    arrive(far_in.at[1], far_send.at[1], far_recv.at[1], mirror)
    far = wide(far_in[1])
    rows[1] = jnp.concatenate([wide(saved[0, 0, 0]), far[:8]], axis=0)
    put_block(NA, normed(rows[1]))
    rows[2] = jnp.concatenate([wide(saved[1, 0, 0]), far[8:]], axis=0)
    put_block(NB, normed(rows[2]))
    gather_outer(FA)
    gather_inner(NA)
    gather_inner(GA)
    gather_relay(FA)
    gather_outer(NA)
    gather_end(FA)
    for load in loads:
        load.wait()
    forward(0, FA)
    gather_relay(NA)
    gather_outer(GA)
    scatter_relay(0)
    gather_end(NA)
    backward_hidden(0, NA)
    gather_relay(GA)
    gather_inner(NB)
    scatter_inner(0)
    gather_end(GA)
    backward(1, 0, GA)
    gather_outer(NB)
    produced = (rows[0] + scatter_end(0)).astype(BF16)
    hop(0, produced, after)
    deliver(0, states_out, 0, produced)
    backward_keep(0)
    gather_relay(NB)
    rows[3] = jnp.where(s == 0, joined(entering[0, 0], entering[0, 1]), hopped(0, after))
    put_block(FB, normed(rows[3]))
    gather_inner(FB)
    scatter_relay(1)
    gather_outer(FB)
    gather_end(NB)
    backward_hidden(1, NB)
    scatter_inner(1)
    gather_relay(FB)

    def returned(n, cot, p):
        scaled = scatter_end(p) * gain
        factor = factor_of(rows[n])
        unit = rows[n] * factor
        return (cot + factor * (scaled - unit * mean(unit * scaled))).astype(BF16)

    back = returned(1, grads[0], 1)
    hop(1, back, before)
    deliver(1, input_grads, 0, back)
    gather_end(FB)
    forward(2, FB)
    grads[1] = jnp.where(
        s == sections - 1, joined(cot_entering[0, 0], cot_entering[0, 1]), hopped(1, before)
    )
    put_block(GB, grads[1])
    gather_inner(GB)
    scatter_relay(2)
    gather_outer(GB)
    gather_relay(GB)
    scatter_inner(2)
    gather_end(GB)
    backward(3, 1, GB)
    produced = (rows[3] + scatter_end(2)).astype(BF16)
    deliver(2, states_out, 1, produced)
    stores = [weight_grad(1, 0, grad_down, GA, GB)]
    scatter_relay(3)
    stores.append(weight_grad(1, 1, grad_down, GA, GB))
    backward_keep(1)
    stores.append(weight_grad(0, 0, grad_up, NA, NB))
    scatter_inner(3)
    stores.append(weight_grad(0, 1, grad_up, NA, NB))
    back = returned(2, grads[1], 3)
    deliver(3, input_grads, 1, back)
    for n, target, period in (
        (0, states_out, 0), (1, input_grads, 0), (2, states_out, 1), (3, input_grads, 1),
    ):
        delivered(n, target, period)
    for copy in stores:
        copy.wait()
    for copy in sends:
        copy.wait_send()


def body(states_in, entering, saved, cotangent, cot_entering, gains, up_rows, down_rows):
    units, features = up_rows.shape[2:]
    width = features // 2
    dma, vmem = pltpu.SemaphoreType.DMA, pltpu.VMEM
    in_vmem = pl.BlockSpec(memory_space=pltpu.VMEM)
    anywhere = pl.BlockSpec(memory_space=pl.ANY)
    grid_rows = (RING, RING, 16, width)
    return pl.pallas_call(
        kernel,
        out_shape=(
            jax.ShapeDtypeStruct(saved.shape, BF16),
            jax.ShapeDtypeStruct(saved.shape, BF16),
            jax.ShapeDtypeStruct((1, units, features), BF16),
            jax.ShapeDtypeStruct((1, units, features), BF16),
        ),
        in_specs=[in_vmem] * 6 + [anywhere] * 2,
        out_specs=(in_vmem, in_vmem, anywhere, anywhere),
        scratch_shapes=[
            vmem((2, units, width), BF16),
            vmem((2, units, width), BF16),
            vmem((6, 2) + grid_rows, BF16),
            vmem((4, 2) + grid_rows, BF16),
            vmem((4, 2) + grid_rows[1:], BF16),
            vmem((4, 2) + grid_rows[1:], BF16),
            vmem((4, 2) + grid_rows[1:], BF16),
            vmem((4, 2) + grid_rows[1:], BF16),
            vmem((4, 2, 3, 16, width), BF16),
            vmem((4, 16, features), F32),
            vmem((2, 16, features), F32),
            vmem((2, 16, features), BF16),
            vmem((2, 16, features), BF16),
            vmem((2, 16, features), BF16),
            vmem((2, 16, features), BF16),
            vmem((4, 16, features), BF16),
            vmem((4, 16, features), BF16),
            vmem((256, units), BF16),
            vmem((256, units), F32),
            vmem((256, units), BF16),
            vmem((2, 2, units, 256), BF16),
            vmem((2, 2, units, width), BF16),
            dma((4,)),
            dma((2, 2)),
            dma((6, 2, 7)),
            dma((6, 2, 7)),
            dma((4, 2, 9)),
            dma((4, 2, 9)),
            dma((2,)),
            dma((2,)),
            dma((2,)),
            dma((2,)),
            dma((4,)),
            dma((4,)),
        ],
        compiler_params=pltpu.CompilerParams(
            collective_id=0, has_side_effects=True, vmem_limit_bytes=60 * 2**20
        ),
        cost_estimate=pl.CostEstimate(flops=15 * 10**9, bytes_accessed=17 * 10**6, transcendentals=0),
    )(states_in, entering, saved, cotangent, cot_entering, gains, up_rows, down_rows)


def solution(mesh):
    group = ("dp", "tensor")
    placed = (
        P(None, "section", group, None),
        P(None, None, group, None),
        P(None, None, "section", group, None),
        P(None, "section", group, None),
        P(None, None, group, None),
        P(),
        P("section", None, group, None),
        P("section", None, group, None),
    )
    return jax.shard_map(
        body,
        mesh=mesh,
        in_specs=placed,
        out_specs=(
            P(None, None, "section", group, None),
            P(None, None, "section", group, None),
            P("section", group, None),
            P("section", group, None),
        ),
        check_vma=False,
    )
```

time: 628 us -> 162 us (0.26)
  waiting for transfers between devices: 470 us -> 0 us
  Pallas kernels: 0 us -> 151 us
  starting transfers between devices: 71.6 us -> 0 us
  matrix products: 59.6 us -> 0 us
  between operations: 14.3 us -> 0.64 us
  other arithmetic: 7.68 us -> 0 us
  local copies, waits for them, and re-layouts: 3.43 us -> 9.85 us
    all_gather x6 -> x0, waiting for transfers between devices: 403 us -> none  [gather(): return lax.all_gather(block, GROUP, axis=0, tiled=True)]
    pallas_call x0 -> x1, Pallas kernels: none -> 151 us  [body(): pl.pallas_call(kernel, out_shape=(jax.ShapeDtypeStruct(saved.shape, BF16)...]
    dot_general x10 -> x0, matrix products: 59.6 us -> none  [the longest x2 20.3 us: body(): out = jnp.dot(acted, down, preferred_element_type=jnp.float32)]
    all_to_all x4 -> x0, waiting for transfers between devices: 55.4 us -> none  [spread_sum(): lax.all_to_all(blocks, GROUP, split_axis=0, concat_axis=0, tiled=True)]
    ppermute x4 -> x0, starting transfers between devices: 49.5 us -> none  [the longest x1 15.8 us: body(): lax.ppermute(produced, 'section', [(i, i + 1) for i in range(sections - 1)])]
    all_to_all x4 -> x0, starting transfers between devices: 21.9 us -> none  [spread_sum(): lax.all_to_all(blocks, GROUP, split_axis=0, concat_axis=0, tiled=True)]
    ppermute x4 -> x0, waiting for transfers between devices: 10.9 us -> none  [the longest x1 4.85 us: body(): far = lax.ppermute(far, 'section', mirror)]
    unnamed x16 -> x6, local copies, waits for them, and re-layouts: 0.73 us -> 9.85 us
  transfers between devices with their start and end apart: 14 -> 0, of which waited for: 14 -> 0; matrix products, arithmetic and copies ran while one was open for 4% -> 0% of each run, Pallas kernels for 0% -> 0%
where the time goes in v2:
time: 162 us
  Pallas kernels  151 us (93%)
  local copies, waits for them, and re-layouts  9.85 us (6%)
    pallas_call x1, Pallas kernels, body(): pl.pallas_call(kernel, out_shape=(jax.ShapeDtypeStruct(saved.shape, BF16)...  151 us
    unnamed x6, local copies, waits for them, and re-layouts  9.85 us

profile of v2, /device:TPU:1, one launch (start us, length us, event | category | flops | bytes accessed | tf_op | source)
XLA Modules:
  0.0 161.9 jit_solution(15225101022349339012)
XLA Ops:
  0.6 151.4 %shard_map.111 = (bf16[2,2,1,8,3584]{4,3,2,1,0:T(8,128)(2,1)}, bf16[2,2,1,8,3584]{4,3,2,1,0:T(8,128)(2,1)}, bf16[1,576,3584]{2,1,0:T(8,128)(2,1)}, bf16[1,576,3584]{2,1,0:T(8,128)(2,1)}) custom-call(bf16[2,1,8,3584]{3,2,1,0:T(8,128)(2,1)} %states_in.1, bf16[1,2,8,3584]{3,2,1,0:T(8,128)(2,1)} %entering.1, bf16[2,2,1,8,3584]{4,3,2,1,0:T(8,128)(2,1)} %saved.1, ...), custom_call_target="tpu_custom_call" | custom-call | flops 15000000512 | bytes 17000000 | tf_op jit(solution)/shard_map/pallas_call | solution.py:382
  152.0 1.6 %copy.16 = bf16[2,2,1,8,3584]{4,3,2,1,0:T(8,128)(2,1)} copy(bf16[2,2,1,8,3584]{4,3,2,1,0:T(8,128)(2,1)} %get-tuple-element.8) | data formatting | bytes 458752
  153.7 1.6 %copy.17 = bf16[2,2,1,8,3584]{4,3,2,1,0:T(8,128)(2,1)} copy(bf16[2,2,1,8,3584]{4,3,2,1,0:T(8,128)(2,1)} %get-tuple-element.9) | data formatting | bytes 458752
  155.3 0.0 copy-start
  155.3 4.6 %copy.18 = bf16[1,576,3584]{2,1,0:T(8,128)(2,1)} copy(bf16[1,576,3584]{2,1,0:T(8,128)(2,1)} %get-tuple-element.10) | data formatting | bytes 8257536
  159.9 0.0 copy-done
  159.9 2.0 %copy.19 = bf16[1,576,3584]{2,1,0:T(8,128)(2,1)} copy(bf16[1,576,3584]{2,1,0:T(8,128)(2,1)S(1)} %copy-done) | data formatting | bytes 8257536
Async XLA Ops:
  155.3 4.6 %copy-start = (bf16[1,576,3584]{2,1,0:T(8,128)(2,1)S(1)}, bf16[1,576,3584]{2,1,0:T(8,128)(2,1)}, u32[]{:S(2)}) copy-start(bf16[1,576,3584]{2,1,0:T(8,128)(2,1)} %get-tuple-element.11) | copy-start | bytes 12386308

commit v3 on v2

--- a/solution.py
+++ b/solution.py
@@ -27,8 +27,8 @@
     states_out, input_grads, grad_up, grad_down,
     up, down, gathered, partial, pass_on, from_prev, from_next, summed, scattered,
     rows, grads, far_out, far_in, hop_out, hop_in, mirror_out, mirror_in,
-    slopes, hidden_kept, active_kept, flipped, staged,
-    load_sem, store_sem, ag_send, ag_recv, rs_send, rs_recv, far_send, far_recv,
+    slopes, hidden_kept, active_kept, flipped,
+    load_sem, ag_send, ag_recv, rs_send, rs_recv, far_send, far_recv,
     hop_send, hop_recv, mirror_send, mirror_recv,
 ):
     s = lax.axis_index("section")
@@ -201,13 +201,10 @@
     def onto_features(p, value, weights):
         tile = 256
         for h in range(2):
-            def one(n, carry):
-                lanes = pl.ds(pl.multiple_of(n * tile, tile), tile)
+            for n in range(width // tile):
+                lanes = pl.ds(n * tile, tile)
                 product = jnp.dot(value, weights[h, :, lanes], preferred_element_type=F32)
                 partial[p, h, :, :, :, lanes] = product.astype(BF16).reshape(RING, RING, 16, tile)
-                return carry
-
-            lax.fori_loop(0, width // tile, one, 0)
             scatter_start(p, h)
 
     def forward(p, a):
@@ -231,23 +228,14 @@
 
     def weight_grad(kind, h, target, first, second):
         tile = 256
-
-        def one(n, carry):
-            lanes = pl.ds(pl.multiple_of(n * tile, tile), tile)
-            total = jnp.dot(
-                flipped[kind, 0], gathered[first, h, :, :, :, lanes].reshape(-1, tile), preferred_element_type=F32
-            ) + jnp.dot(
-                flipped[kind, 1], gathered[second, h, :, :, :, lanes].reshape(-1, tile), preferred_element_type=F32
+        left = jnp.concatenate([flipped[kind, 0], flipped[kind, 1]], axis=1)
+        for n in range(width // tile):
+            lanes = pl.ds(n * tile, tile)
+            right = jnp.concatenate(
+                [gathered[a, h, :, :, :, lanes].reshape(-1, tile) for a in (first, second)], axis=0
             )
-            staged[kind, h, :, lanes] = total.astype(BF16)
-            return carry
-
-        lax.fori_loop(0, width // tile, one, 0)
-        copy = pltpu.make_async_copy(
-            staged.at[kind, h], target.at[0, :, pl.ds(h * width, width)], store_sem.at[kind, h]
-        )
-        copy.start()
-        return copy
+            total = jnp.dot(left, right, preferred_element_type=F32)
+            target[0, :, pl.ds(h * width + n * tile, tile)] = total.astype(BF16)
 
     def hop(n, value, to):
         hop_out[n] = value.astype(BF16)
@@ -353,23 +341,30 @@
     backward(3, 1, GB)
     produced = (rows[3] + scatter_end(2)).astype(BF16)
     deliver(2, states_out, 1, produced)
-    stores = [weight_grad(1, 0, grad_down, GA, GB)]
+    weight_grad(1, 0, grad_down, GA, GB)
     scatter_relay(3)
-    stores.append(weight_grad(1, 1, grad_down, GA, GB))
+    weight_grad(1, 1, grad_down, GA, GB)
     backward_keep(1)
-    stores.append(weight_grad(0, 0, grad_up, NA, NB))
+    weight_grad(0, 0, grad_up, NA, NB)
     scatter_inner(3)
-    stores.append(weight_grad(0, 1, grad_up, NA, NB))
+    weight_grad(0, 1, grad_up, NA, NB)
     back = returned(2, grads[1], 3)
     deliver(3, input_grads, 1, back)
     for n, target, period in (
         (0, states_out, 0), (1, input_grads, 0), (2, states_out, 1), (3, input_grads, 1),
     ):
         delivered(n, target, period)
-    for copy in stores:
-        copy.wait()
     for copy in sends:
         copy.wait_send()
+
+
+def write_out(*refs):
+    sems = refs[-1]
+    copies = [pltpu.make_async_copy(refs[n], refs[4 + n], sems.at[n]) for n in range(4)]
+    for copy in copies:
+        copy.start()
+    for copy in copies:
+        copy.wait()
 
 
 def body(states_in, entering, saved, cotangent, cot_entering, gains, up_rows, down_rows):
@@ -379,16 +374,12 @@
     in_vmem = pl.BlockSpec(memory_space=pltpu.VMEM)
     anywhere = pl.BlockSpec(memory_space=pl.ANY)
     grid_rows = (RING, RING, 16, width)
-    return pl.pallas_call(
+    shapes = (saved.shape, saved.shape, (1, units, features), (1, units, features))
+    results = pl.pallas_call(
         kernel,
-        out_shape=(
-            jax.ShapeDtypeStruct(saved.shape, BF16),
-            jax.ShapeDtypeStruct(saved.shape, BF16),
-            jax.ShapeDtypeStruct((1, units, features), BF16),
-            jax.ShapeDtypeStruct((1, units, features), BF16),
-        ),
+        out_shape=tuple(vmem(shape, BF16) for shape in shapes),
         in_specs=[in_vmem] * 6 + [anywhere] * 2,
-        out_specs=(in_vmem, in_vmem, anywhere, anywhere),
+        out_specs=(in_vmem,) * 4,
         scratch_shapes=[
             vmem((2, units, width), BF16),
             vmem((2, units, width), BF16),
@@ -411,9 +402,7 @@
             vmem((256, units), F32),
             vmem((256, units), BF16),
             vmem((2, 2, units, 256), BF16),
-            vmem((2, 2, units, width), BF16),
             dma((4,)),
-            dma((2, 2)),
             dma((6, 2, 7)),
             dma((6, 2, 7)),
             dma((4, 2, 9)),
@@ -426,10 +415,18 @@
             dma((4,)),
         ],
         compiler_params=pltpu.CompilerParams(
-            collective_id=0, has_side_effects=True, vmem_limit_bytes=60 * 2**20
+            collective_id=0, has_side_effects=True, vmem_limit_bytes=48 * 2**20
         ),
         cost_estimate=pl.CostEstimate(flops=15 * 10**9, bytes_accessed=17 * 10**6, transcendentals=0),
     )(states_in, entering, saved, cotangent, cot_entering, gains, up_rows, down_rows)
+    return pl.pallas_call(
+        write_out,
+        out_shape=tuple(jax.ShapeDtypeStruct(shape, BF16) for shape in shapes),
+        in_specs=[in_vmem] * 4,
+        out_specs=(anywhere,) * 4,
+        scratch_shapes=[dma((4,))],
+        compiler_params=pltpu.CompilerParams(vmem_limit_bytes=4 * 2**20),
+    )(*results)
 
 
 def solution(mesh):

time: 162 us -> 149 us (0.920)
  local copies, waits for them, and re-layouts: 9.85 us -> 0 us
  Pallas kernels: 151 us -> 148 us
    unnamed x6 -> x0, local copies, waits for them, and re-layouts: 9.85 us -> none
    pallas_call x1 -> x2, Pallas kernels: 151 us -> 148 us  [the longest x1 144 us: body(): pl.pallas_call(kernel, out_shape=tuple((vmem(shape, BF16) for shape in sh...]
where the time goes in v3:
time: 149 us
  Pallas kernels  148 us (99%)
    pallas_call x1, Pallas kernels, body(): pl.pallas_call(kernel, out_shape=tuple((vmem(shape, BF16) for shape in sh...  144 us
    pallas_call x1, Pallas kernels, body(): pl.pallas_call(write_out, out_shape=tuple((jax.ShapeDtypeStruct(shape, BF...  3.53 us

profile of v3, /device:TPU:1, one launch (start us, length us, event | category | flops | bytes accessed | tf_op | source)
XLA Modules:
  0.0 148.7 jit_solution(384940168130480004)
XLA Ops:
  0.6 144.3 %shard_map.111 = (bf16[2,2,1,8,3584]{4,3,2,1,0:T(8,128)(2,1)S(1)}, bf16[2,2,1,8,3584]{4,3,2,1,0:T(8,128)(2,1)S(1)}, bf16[1,576,3584]{2,1,0:T(8,128)(2,1)S(1)}, bf16[1,576,3584]{2,1,0:T(8,128)(2,1)S(1)}) custom-call(bf16[2,1,8,3584]{3,2,1,0:T(8,128)(2,1)} %states_in.1, bf16[1,2,8,3584]{3,2,1,0:T(8,128)(2,1)} %entering.1, bf16[2,2,1,8,3584]{4,3,2,1,0:T(8,128)(2,1)} %saved.1, ...), custom_call_target="tpu_custom_call" | custom-call | flops 15000000512 | bytes 17000000 | tf_op jit(solution)/shard_map/pallas_call | solution.py:378
  145.0 3.5 %shard_map.112 = (bf16[2,2,1,8,3584]{4,3,2,1,0:T(8,128)(2,1)}, bf16[2,2,1,8,3584]{4,3,2,1,0:T(8,128)(2,1)}, bf16[1,576,3584]{2,1,0:T(8,128)(2,1)}, bf16[1,576,3584]{2,1,0:T(8,128)(2,1)}) custom-call(bf16[2,2,1,8,3584]{4,3,2,1,0:T(8,128)(2,1)S(1)} %get-tuple-element.8.refs_0_, bf16[2,2,1,8,3584]{4,3,2,1,0:T(8,128)(2,1)S(1)} %get-tuple-element.9.refs_1_, ...), custom_call_target="tpu_custom_call" | custom-call | tf_op jit(solution)/shard_map/pallas_call | solution.py:422

commit v4 on v3

--- a/solution.py
+++ b/solution.py
@@ -11,7 +11,16 @@
 MESH = pl.DeviceIdType.MESH
 F32, BF16 = jnp.float32, jnp.bfloat16
 FA, NA, GA, NB, FB, GB = range(6)
+FS, NS, GS = (FA, FB), (NA, NB), (GA, GB)
 RING = 4
+
+ORDER = (
+    "far0", "far1", "far2", "nF0", "nG0", "nN0", "outF0", "outN0", "relF0", "outG0", "relN0",
+    "relG0", "hF0", "pF0h0", "pF0h1", "hB0", "nN1", "gB0", "rsrF0", "pB0h0", "pB0h1", "rsiF0",
+    "rsrB0", "outN1", "finF0", "rsiB0", "nF1", "relN1", "finB0", "outF1", "nG1", "hB1", "relF1",
+    "outG1", "hF1", "relG1", "pF1h0", "pF1h1", "gB1", "rsrF1", "pB1h0", "pB1h1", "w1a", "keepB1",
+    "rsrB1", "rsiF1", "w1b", "keepB0", "rsiB1", "w0a", "finF1", "finB1", "w0b", "end",
+)
 
 
 def contract_last(former, latter):
@@ -26,8 +35,8 @@
     states_in, entering, saved, cotangent, cot_entering, gains, up_rows, down_rows,
     states_out, input_grads, grad_up, grad_down,
     up, down, gathered, partial, pass_on, from_prev, from_next, summed, scattered,
-    rows, grads, far_out, far_in, hop_out, hop_in, mirror_out, mirror_in,
-    slopes, hidden_kept, active_kept, flipped,
+    rows, far_out, far_in, hop_out, hop_in, mirror_out, mirror_in,
+    slopes, bent, active, flipped,
     load_sem, ag_send, ag_recv, rs_send, rs_recv, far_send, far_recv,
     hop_send, hop_recv, mirror_send, mirror_recv,
 ):
@@ -109,24 +118,25 @@
             for step in (1, 2, 3):
                 sems = (ag_send.at[a, h, step - 1], ag_recv.at[a, h, step - 1])
                 arrive(block(gathered, a, h, -step), *sems, along(inner[h], step))
-            own = slab(gathered, a, h, 0, whole)
-            for n, step in ((3, 1), (4, -1)):
-                send(own, own, ag_send.at[a, h, n], ag_recv.at[a, h, n], along(outer[h], step))
+        for group in (((3, 1, low), (4, -1, high)), ((7, 1, high), (8, -1, low))):
+            for h in range(2):
+                for n, step, lanes in group:
+                    own = slab(gathered, a, h, 0, lanes)
+                    send(own, own, ag_send.at[a, h, n], ag_recv.at[a, h, n], along(outer[h], step))
 
     def gather_relay(a):
         for h in range(2):
             for n, step, lanes in ((3, 1, low), (4, -1, high)):
+                passed = slab(gathered, a, h, -step, lanes)
+                arrive(passed, ag_send.at[a, h, n], ag_recv.at[a, h, n], along(outer[h], step))
+                sems = (ag_send.at[a, h, n + 2], ag_recv.at[a, h, n + 2])
+                send(passed, passed, *sems, along(outer[h], step))
+
+    def gather_end(a):
+        for h in range(2):
+            for n, step, lanes, far in ((5, 1, low, 2), (6, -1, high, 2), (7, 1, high, 1), (8, -1, low, 1)):
                 sems = (ag_send.at[a, h, n], ag_recv.at[a, h, n])
-                arrive(slab(gathered, a, h, -step, whole), *sems, along(outer[h], step))
-                sems = (ag_send.at[a, h, n + 2], ag_recv.at[a, h, n + 2])
-                passed = slab(gathered, a, h, -step, lanes)
-                send(passed, passed, *sems, along(outer[h], step))
-
-    def gather_end(a):
-        for h in range(2):
-            for n, step, lanes in ((5, 1, low), (6, -1, high)):
-                sems = (ag_send.at[a, h, n], ag_recv.at[a, h, n])
-                arrive(slab(gathered, a, h, -2 * step, lanes), *sems, along(outer[h], step))
+                arrive(slab(gathered, a, h, -far * step, lanes), *sems, along(outer[h], step))
 
     def scatter_start(p, h):
         def put(n, step, lanes, target, to):
@@ -198,33 +208,41 @@
     def onto_units(a, weights):
         return contract_last(tokens(a, 0), weights[0]) + contract_last(tokens(a, 1), weights[1])
 
-    def onto_features(p, value, weights):
+    def onto_features(p, h, value, weights):
         tile = 256
-        for h in range(2):
-            for n in range(width // tile):
-                lanes = pl.ds(n * tile, tile)
-                product = jnp.dot(value, weights[h, :, lanes], preferred_element_type=F32)
-                partial[p, h, :, :, :, lanes] = product.astype(BF16).reshape(RING, RING, 16, tile)
-            scatter_start(p, h)
-
-    def forward(p, a):
-        hidden = onto_units(a, up)
-        active = (hidden * jax.nn.sigmoid(hidden)).astype(BF16)
-        onto_features(p, active, down)
-
-    def backward_hidden(period, a):
-        hidden = onto_units(a, up)
+        for n in range(width // tile):
+            lanes = pl.ds(n * tile, tile)
+            product = jnp.dot(value, weights[h, :, lanes], preferred_element_type=F32)
+            partial[p, h, :, :, :, lanes] = product.astype(BF16).reshape(RING, RING, 16, tile)
+        scatter_start(p, h)
+
+    loaded = set()
+
+    def weights_of(n):
+        if n not in loaded:
+            loaded.add(n)
+            for load in loads[2 * n : 2 * n + 2]:
+                load.wait()
+        return (up, down)[n]
+
+    def hidden_forward(period):
+        gather_end(FS[period])
+        hidden = onto_units(FS[period], weights_of(0))
+        active[...] = (hidden * jax.nn.sigmoid(hidden)).astype(BF16)
+
+    def hidden_backward(period):
+        gather_end(NS[period])
+        hidden = onto_units(NS[period], weights_of(0))
         gating = jax.nn.sigmoid(hidden)
-        active_kept[...] = (hidden * gating).astype(BF16)
-        hidden_kept[...] = gating * (1.0 + hidden * (1.0 - gating))
-        flipped[1, period] = active_kept[...].T
-
-    def backward(p, period, a):
-        slopes[...] = (onto_units(a, down) * hidden_kept[...]).astype(BF16)
-        onto_features(p, slopes[...], up)
-
-    def backward_keep(period):
-        flipped[0, period] = slopes[...].T
+        flipped[1, period] = (hidden * gating).astype(BF16).T
+        bent[period] = gating * (1.0 + hidden * (1.0 - gating))
+
+    def slope(period):
+        gather_end(GS[period])
+        slopes[period] = (onto_units(GS[period], weights_of(1)) * bent[period]).astype(BF16)
+
+    def keep_slope(period):
+        flipped[0, period] = slopes[period].T
 
     def weight_grad(kind, h, target, first, second):
         tile = 256
@@ -237,125 +255,125 @@
             total = jnp.dot(left, right, preferred_element_type=F32)
             target[0, :, pl.ds(h * width + n * tile, tile)] = total.astype(BF16)
 
+    def wide(value):
+        return value.astype(F32)
+
+    def folded(value):
+        return jnp.concatenate([wide(value)[:, :width], wide(value)[:, width:]], axis=0).astype(BF16)
+
+    def unfolded(value):
+        return jnp.concatenate([wide(value)[:8], wide(value)[8:]], axis=1)
+
+    def far_send_one(n, value):
+        far_out[n] = folded(value)
+        send(far_out.at[n], far_in.at[n], far_send.at[n], far_recv.at[n], mirror)
+
+    def with_far(own, n):
+        arrive(far_in.at[n], far_send.at[n], far_recv.at[n], mirror)
+        return jnp.concatenate([wide(own), unfolded(far_in[n])], axis=0)
+
     def hop(n, value, to):
-        hop_out[n] = value.astype(BF16)
+        hop_out[n] = value
         send(hop_out.at[n], hop_in.at[n], hop_send.at[n], hop_recv.at[n], to)
 
     def hopped(n, to):
         arrive(hop_in.at[n], hop_send.at[n], hop_recv.at[n], to)
-        return hop_in[n].astype(F32)
+        return wide(hop_in[n])
 
     def deliver(n, target, period, value):
-        value = value.astype(BF16)
-        mirror_out[n] = value
+        mirror_out[n] = folded(value[8:])
         send(mirror_out.at[n], mirror_in.at[n], mirror_send.at[n], mirror_recv.at[n], mirror)
-        target[period, 0, 0] = value.astype(F32)[:8].astype(BF16)
+        target[period, 0, 0] = value[:8].astype(BF16)
 
     def delivered(n, target, period):
         arrive(mirror_in.at[n], mirror_send.at[n], mirror_recv.at[n], mirror)
-        target[period, 1, 0] = mirror_in[n].astype(F32)[8:].astype(BF16)
-
-    def wide(value):
-        return value.astype(F32)
-
-    def joined(first, second):
-        return jnp.concatenate([wide(first), wide(second)], axis=0)
-
-    far_out[0] = joined(states_in[1, 0], cotangent[1, 0]).astype(BF16)
-    send(far_out.at[0], far_in.at[0], far_send.at[0], far_recv.at[0], mirror)
-    far_out[1] = joined(saved[0, 1, 0], saved[1, 1, 0]).astype(BF16)
-    send(far_out.at[1], far_in.at[1], far_send.at[1], far_recv.at[1], mirror)
+        target[period, 1, 0] = unfolded(mirror_in[n]).astype(BF16)
+
+    def rounded(value):
+        return wide(value.astype(BF16))
+
+    def finish_forward(period):
+        p = 2 * period
+        produced = rounded(rows[FS[period]] + scatter_end(p))
+        if period == 0:
+            hop(0, produced.astype(BF16), after)
+        deliver(p, states_out, period, produced)
+
+    def finish_backward(period):
+        p = 2 * period + 1
+        scaled = scatter_end(p) * gain
+        own = rows[NS[period]]
+        factor = factor_of(own)
+        unit = own * factor
+        back = factor * (scaled - unit * mean(unit * scaled))
+        back = rounded(rows[GS[period]] + back)
+        if period == 0:
+            hop(1, back.astype(BF16), before)
+        deliver(p, input_grads, period, back)
+
+    def begin(a, value):
+        rows[a] = value
+        put_block(a, value if a in GS else normed(value))
+        gather_inner(a)
+
+    def joined(pair):
+        return jnp.concatenate([wide(pair[0]), wide(pair[1])], axis=0)
+
+    def begin_later_forward():
+        begin(FB, jnp.where(s == 0, joined(entering[0]), hopped(0, after)))
+
+    def begin_later_grads():
+        begin(GB, jnp.where(s == sections - 1, joined(cot_entering[0]), hopped(1, before)))
+
+    def far_saved():
+        far_send_one(2, saved[0, 1, 0])
+        far_send_one(3, saved[1, 1, 0])
+
+    def end():
+        for n, target in enumerate((states_out, input_grads) * 2):
+            delivered(n, target, n // 2)
+        for copy in sends:
+            copy.wait_send()
 
     chosen = lax.broadcasted_iota(jnp.int32, gains.shape, 0) == s
     gain = jnp.sum(jnp.where(chosen, wide(gains[...]), 0.0), axis=0, keepdims=True)
-
-    arrive(far_in.at[0], far_send.at[0], far_recv.at[0], mirror)
-    far = wide(far_in[0])
-    rows[0] = jnp.concatenate([wide(states_in[0, 0]), far[:8]], axis=0)
-    put_block(FA, normed(rows[0]))
-    gather_inner(FA)
-    grads[0] = jnp.concatenate([wide(cotangent[0, 0]), far[8:]], axis=0)
-    put_block(GA, grads[0])
-    arrive(far_in.at[1], far_send.at[1], far_recv.at[1], mirror)
-    far = wide(far_in[1])
-    rows[1] = jnp.concatenate([wide(saved[0, 0, 0]), far[:8]], axis=0)
-    put_block(NA, normed(rows[1]))
-    rows[2] = jnp.concatenate([wide(saved[1, 0, 0]), far[8:]], axis=0)
-    put_block(NB, normed(rows[2]))
-    gather_outer(FA)
-    gather_inner(NA)
-    gather_inner(GA)
-    gather_relay(FA)
-    gather_outer(NA)
-    gather_end(FA)
-    for load in loads:
-        load.wait()
-    forward(0, FA)
-    gather_relay(NA)
-    gather_outer(GA)
-    scatter_relay(0)
-    gather_end(NA)
-    backward_hidden(0, NA)
-    gather_relay(GA)
-    gather_inner(NB)
-    scatter_inner(0)
-    gather_end(GA)
-    backward(1, 0, GA)
-    gather_outer(NB)
-    produced = (rows[0] + scatter_end(0)).astype(BF16)
-    hop(0, produced, after)
-    deliver(0, states_out, 0, produced)
-    backward_keep(0)
-    gather_relay(NB)
-    rows[3] = jnp.where(s == 0, joined(entering[0, 0], entering[0, 1]), hopped(0, after))
-    put_block(FB, normed(rows[3]))
-    gather_inner(FB)
-    scatter_relay(1)
-    gather_outer(FB)
-    gather_end(NB)
-    backward_hidden(1, NB)
-    scatter_inner(1)
-    gather_relay(FB)
-
-    def returned(n, cot, p):
-        scaled = scatter_end(p) * gain
-        factor = factor_of(rows[n])
-        unit = rows[n] * factor
-        return (cot + factor * (scaled - unit * mean(unit * scaled))).astype(BF16)
-
-    back = returned(1, grads[0], 1)
-    hop(1, back, before)
-    deliver(1, input_grads, 0, back)
-    gather_end(FB)
-    forward(2, FB)
-    grads[1] = jnp.where(
-        s == sections - 1, joined(cot_entering[0, 0], cot_entering[0, 1]), hopped(1, before)
-    )
-    put_block(GB, grads[1])
-    gather_inner(GB)
-    scatter_relay(2)
-    gather_outer(GB)
-    gather_relay(GB)
-    scatter_inner(2)
-    gather_end(GB)
-    backward(3, 1, GB)
-    produced = (rows[3] + scatter_end(2)).astype(BF16)
-    deliver(2, states_out, 1, produced)
-    weight_grad(1, 0, grad_down, GA, GB)
-    scatter_relay(3)
-    weight_grad(1, 1, grad_down, GA, GB)
-    backward_keep(1)
-    weight_grad(0, 0, grad_up, NA, NB)
-    scatter_inner(3)
-    weight_grad(0, 1, grad_up, NA, NB)
-    back = returned(2, grads[1], 3)
-    deliver(3, input_grads, 1, back)
-    for n, target, period in (
-        (0, states_out, 0), (1, input_grads, 0), (2, states_out, 1), (3, input_grads, 1),
-    ):
-        delivered(n, target, period)
-    for copy in sends:
-        copy.wait_send()
+    steps = {
+        "far0": lambda: far_send_one(0, states_in[1, 0]),
+        "far1": lambda: far_send_one(1, cotangent[1, 0]),
+        "far2": far_saved,
+        "nF0": lambda: begin(FA, with_far(states_in[0, 0], 0)),
+        "nG0": lambda: begin(GA, with_far(cotangent[0, 0], 1)),
+        "nN0": lambda: begin(NA, with_far(saved[0, 0, 0], 2)),
+        "nN1": lambda: begin(NB, with_far(saved[1, 0, 0], 3)),
+        "nF1": begin_later_forward,
+        "nG1": begin_later_grads,
+        "w1a": lambda: weight_grad(1, 0, grad_down, GA, GB),
+        "w1b": lambda: weight_grad(1, 1, grad_down, GA, GB),
+        "w0a": lambda: weight_grad(0, 0, grad_up, NA, NB),
+        "w0b": lambda: weight_grad(0, 1, grad_up, NA, NB),
+        "end": end,
+    }
+    for a, name in enumerate(("F0", "N0", "G0", "N1", "F1", "G1")):
+        steps["out" + name] = functools.partial(gather_outer, a)
+        steps["rel" + name] = functools.partial(gather_relay, a)
+    for period in range(2):
+        k = str(period)
+        steps["hF" + k] = functools.partial(hidden_forward, period)
+        steps["hB" + k] = functools.partial(hidden_backward, period)
+        steps["gB" + k] = functools.partial(slope, period)
+        steps["keepB" + k] = functools.partial(keep_slope, period)
+        steps["finF" + k] = functools.partial(finish_forward, period)
+        steps["finB" + k] = functools.partial(finish_backward, period)
+        for h in range(2):
+            steps[f"pF{k}h{h}"] = lambda p=2 * period, h=h: onto_features(p, h, active[...], weights_of(1))
+            steps[f"pB{k}h{h}"] = lambda p=2 * period + 1, h=h: onto_features(
+                p, h, slopes[p // 2], weights_of(0)
+            )
+        for n, name in enumerate("FB"):
+            steps["rsr" + name + k] = functools.partial(scatter_relay, 2 * period + n)
+            steps["rsi" + name + k] = functools.partial(scatter_inner, 2 * period + n)
+    for name in ORDER:
+        steps[name]()
 
 
 def write_out(*refs):
@@ -390,25 +408,24 @@
             vmem((4, 2) + grid_rows[1:], BF16),
             vmem((4, 2) + grid_rows[1:], BF16),
             vmem((4, 2, 3, 16, width), BF16),
-            vmem((4, 16, features), F32),
-            vmem((2, 16, features), F32),
+            vmem((6, 16, features), F32),
+            vmem((4, 16, width), BF16),
+            vmem((4, 16, width), BF16),
             vmem((2, 16, features), BF16),
             vmem((2, 16, features), BF16),
-            vmem((2, 16, features), BF16),
-            vmem((2, 16, features), BF16),
-            vmem((4, 16, features), BF16),
-            vmem((4, 16, features), BF16),
-            vmem((256, units), BF16),
-            vmem((256, units), F32),
+            vmem((4, 16, width), BF16),
+            vmem((4, 16, width), BF16),
+            vmem((2, 256, units), BF16),
+            vmem((2, 256, units), F32),
             vmem((256, units), BF16),
             vmem((2, 2, units, 256), BF16),
             dma((4,)),
-            dma((6, 2, 7)),
-            dma((6, 2, 7)),
+            dma((6, 2, 9)),
+            dma((6, 2, 9)),
             dma((4, 2, 9)),
             dma((4, 2, 9)),
-            dma((2,)),
-            dma((2,)),
+            dma((4,)),
+            dma((4,)),
             dma((2,)),
             dma((2,)),
             dma((4,)),

time: 149 us -> 128 us (0.86)
  Pallas kernels: 148 us -> 127 us
    pallas_call x1, Pallas kernels: 144 us -> 124 us  [body(): pl.pallas_call(kernel, out_shape=tuple((vmem(shape, BF16) for shape in sh...]
where the time goes in v4:
time: 128 us
  Pallas kernels  127 us (99%)
    pallas_call x1, Pallas kernels, body(): pl.pallas_call(kernel, out_shape=tuple((vmem(shape, BF16) for shape in sh...  124 us
    pallas_call x1, Pallas kernels, body(): pl.pallas_call(write_out, out_shape=tuple((jax.ShapeDtypeStruct(shape, BF...  3.53 us

profile of v4, /device:TPU:1, one launch (start us, length us, event | category | flops | bytes accessed | tf_op | source)
XLA Modules:
  0.0 128.1 jit_solution(7683769783123978254)
XLA Ops:
  0.6 123.8 %shard_map.111 = (bf16[2,2,1,8,3584]{4,3,2,1,0:T(8,128)(2,1)S(1)}, bf16[2,2,1,8,3584]{4,3,2,1,0:T(8,128)(2,1)S(1)}, bf16[1,576,3584]{2,1,0:T(8,128)(2,1)S(1)}, bf16[1,576,3584]{2,1,0:T(8,128)(2,1)S(1)}) custom-call(bf16[2,1,8,3584]{3,2,1,0:T(8,128)(2,1)} %states_in.1, bf16[1,2,8,3584]{3,2,1,0:T(8,128)(2,1)} %entering.1, bf16[2,2,1,8,3584]{4,3,2,1,0:T(8,128)(2,1)} %saved.1, ...), custom_call_target="tpu_custom_call" | custom-call | flops 15000000512 | bytes 17000000 | tf_op jit(solution)/shard_map/pallas_call | solution.py:396
  124.4 3.5 %shard_map.112 = (bf16[2,2,1,8,3584]{4,3,2,1,0:T(8,128)(2,1)}, bf16[2,2,1,8,3584]{4,3,2,1,0:T(8,128)(2,1)}, bf16[1,576,3584]{2,1,0:T(8,128)(2,1)}, bf16[1,576,3584]{2,1,0:T(8,128)(2,1)}) custom-call(bf16[2,2,1,8,3584]{4,3,2,1,0:T(8,128)(2,1)S(1)} %get-tuple-element.8.refs_0_, bf16[2,2,1,8,3584]{4,3,2,1,0:T(8,128)(2,1)S(1)} %get-tuple-element.9.refs_1_, ...), custom_call_target="tpu_custom_call" | custom-call | tf_op jit(solution)/shard_map/pallas_call | solution.py:439

commit v5 on v4

--- a/solution.py
+++ b/solution.py
@@ -53,10 +53,15 @@
     def device(section, x, z):
         return (section, (z // 2) * RING + x, z % 2)
 
+    def moved(axis, step):
+        to = dict(place)
+        to[axis] = (place[axis] + step) % RING
+        return device(s, to["x"], to["z"])
+
+    neighbours = {(axis, step): moved(axis, step) for axis in "xz" for step in (1, 2, 3)}
+
     def along(axis, step):
-        moved = dict(place)
-        moved[axis] = (place[axis] + step) % RING
-        return device(s, moved["x"], moved["z"])
+        return neighbours[axis, step % RING]
 
     mirror = device(sections - 1 - s, place["x"], place["z"])
     after = device((s + 1) % sections, place["x"], place["z"])
@@ -78,21 +83,25 @@
         pl.semaphore_signal(barrier, inc=1, device_id=partner, device_id_type=MESH)
     pl.semaphore_wait(barrier, len(partners))
 
-    sends = []
-
     def send(source, target, send_sem, recv_sem, device_id):
-        copy = pltpu.make_async_remote_copy(
+        pltpu.make_async_remote_copy(
             src_ref=source, dst_ref=target, send_sem=send_sem, recv_sem=recv_sem,
             device_id=device_id, device_id_type=MESH,
-        )
-        copy.start()
-        sends.append(copy)
-
-    def arrive(target, send_sem, recv_sem, device_id):
+        ).start()
+
+    def arrived(like, recv_sem):
         pltpu.make_async_remote_copy(
-            src_ref=target, dst_ref=target, send_sem=send_sem, recv_sem=recv_sem,
-            device_id=device_id, device_id_type=MESH,
+            src_ref=like, dst_ref=like, send_sem=recv_sem, recv_sem=recv_sem,
+            device_id=mirror, device_id_type=MESH,
         ).wait_recv()
+
+    def departed(like, send_sem):
+        pltpu.make_async_remote_copy(
+            src_ref=like, dst_ref=like, send_sem=send_sem, recv_sem=send_sem,
+            device_id=mirror, device_id_type=MESH,
+        ).wait_send()
+
+    blocks = {6: scattered.at[0], 8: from_prev.at[0], 16: from_prev.at[0:2], 24: from_prev.at[0:3]}
 
     inner, outer = ("x", "z"), ("z", "x")
     low, high, whole = pl.ds(0, half), pl.ds(half, half), pl.ds(0, width)
@@ -107,68 +116,56 @@
         return ref.at[index, h, at["z"], at["x"]]
 
     def gather_inner(a):
-        for h in range(2):
-            for step in (1, 3, 2):
+        for step in (1, 3, 2):
+            for h in range(2):
                 own = block(gathered, a, h, 0)
-                sems = (ag_send.at[a, h, step - 1], ag_recv.at[a, h, step - 1])
-                send(own, own, *sems, along(inner[h], step))
+                send(own, own, ag_send.at[a, 0], ag_recv.at[a, 0], along(inner[h], step))
 
     def gather_outer(a):
-        for h in range(2):
-            for step in (1, 2, 3):
-                sems = (ag_send.at[a, h, step - 1], ag_recv.at[a, h, step - 1])
-                arrive(block(gathered, a, h, -step), *sems, along(inner[h], step))
-        for group in (((3, 1, low), (4, -1, high)), ((7, 1, high), (8, -1, low))):
+        arrived(blocks[6], ag_recv.at[a, 0])
+        for n, group in ((1, ((1, low), (-1, high))), (2, ((1, high), (-1, low)))):
             for h in range(2):
-                for n, step, lanes in group:
+                for step, lanes in group:
                     own = slab(gathered, a, h, 0, lanes)
-                    send(own, own, ag_send.at[a, h, n], ag_recv.at[a, h, n], along(outer[h], step))
+                    send(own, own, ag_send.at[a, 1], ag_recv.at[a, n], along(outer[h], step))
 
     def gather_relay(a):
-        for h in range(2):
-            for n, step, lanes in ((3, 1, low), (4, -1, high)):
+        arrived(blocks[8], ag_recv.at[a, 1])
+        for h in range(2):
+            for step, lanes in ((1, low), (-1, high)):
                 passed = slab(gathered, a, h, -step, lanes)
-                arrive(passed, ag_send.at[a, h, n], ag_recv.at[a, h, n], along(outer[h], step))
-                sems = (ag_send.at[a, h, n + 2], ag_recv.at[a, h, n + 2])
-                send(passed, passed, *sems, along(outer[h], step))
+                send(passed, passed, ag_send.at[a, 1], ag_recv.at[a, 2], along(outer[h], step))
 
     def gather_end(a):
-        for h in range(2):
-            for n, step, lanes, far in ((5, 1, low, 2), (6, -1, high, 2), (7, 1, high, 1), (8, -1, low, 1)):
-                sems = (ag_send.at[a, h, n], ag_recv.at[a, h, n])
-                arrive(slab(gathered, a, h, -far * step, lanes), *sems, along(outer[h], step))
+        arrived(blocks[16], ag_recv.at[a, 2])
 
     def scatter_start(p, h):
-        def put(n, step, lanes, target, to):
+        for n, step, lanes, target, to in (
+            (0, 2, low, pass_on, 1),
+            (0, 2, high, pass_on, -1),
+            (1, 1, high, from_prev, 1),
+            (1, -1, low, from_next, -1),
+        ):
             send(
                 slab(partial, p, h, step, lanes), target.at[p, h, :, :, lanes],
-                rs_send.at[p, h, n], rs_recv.at[p, h, n], along(outer[h], to),
+                rs_send.at[p, 1], rs_recv.at[p, n], along(outer[h], to),
             )
 
-        put(0, 2, low, pass_on, 1)
-        put(1, 2, high, pass_on, -1)
-        put(2, 1, high, from_prev, 1)
-        put(3, -1, low, from_next, -1)
-
     def scatter_relay(p):
-        for h in range(2):
-            for n, step, lanes, target in ((0, 1, low, from_prev), (1, -1, high, from_next)):
-                passing = pass_on.at[p, h, :, :, lanes]
-                arrive(passing, rs_send.at[p, h, n], rs_recv.at[p, h, n], along(outer[h], step))
+        arrived(blocks[8], rs_recv.at[p, 0])
+        for h in range(2):
+            for step, lanes, target in ((1, low, from_prev), (-1, high, from_next)):
                 mine = slab(partial, p, h, step, lanes)
-                mine[...] = (mine[...].astype(F32) + passing[...].astype(F32)).astype(BF16)
+                passing = pass_on[p, h, :, :, lanes].astype(F32)
+                mine[...] = (mine[...].astype(F32) + passing).astype(BF16)
                 send(
                     mine, target.at[p, h, :, :, lanes],
-                    rs_send.at[p, h, n + 4], rs_recv.at[p, h, n + 4], along(outer[h], step),
+                    rs_send.at[p, 1], rs_recv.at[p, 1], along(outer[h], step),
                 )
 
     def scatter_inner(p):
-        for h in range(2):
-            for n, lanes, target, step in (
-                (2, high, from_prev, 1), (3, low, from_next, -1), (4, low, from_prev, 1), (5, high, from_next, -1),
-            ):
-                landed = target.at[p, h, :, :, lanes]
-                arrive(landed, rs_send.at[p, h, n], rs_recv.at[p, h, n], along(outer[h], step))
+        arrived(blocks[16], rs_recv.at[p, 1])
+        for h in range(2):
             total = slab(partial, p, h, 0, whole)[...].astype(F32)
             total = total + from_prev[p, h].astype(F32) + from_next[p, h].astype(F32)
             summed[p, h] = total.astype(BF16)
@@ -176,18 +173,16 @@
                 at = (place[inner[h]] + step) % RING
                 send(
                     summed.at[p, h, at], scattered.at[p, h, step - 1],
-                    rs_send.at[p, h, 5 + step], rs_recv.at[p, h, 5 + step], along(inner[h], step),
+                    rs_send.at[p, 0], rs_recv.at[p, 2], along(inner[h], step),
                 )
 
     def scatter_end(p):
+        arrived(blocks[6], rs_recv.at[p, 2])
         halves = []
         for h in range(2):
             total = summed[p, h, pl.ds(place[inner[h]], 1)][0].astype(F32)
             for step in (1, 2, 3):
-                landed = scattered.at[p, h, step - 1]
-                sems = (rs_send.at[p, h, 5 + step], rs_recv.at[p, h, 5 + step])
-                arrive(landed, *sems, along(inner[h], step))
-                total = total + landed[...].astype(F32)
+                total = total + scattered[p, h, step - 1].astype(F32)
             halves.append(total)
         return jnp.concatenate(halves, axis=1)
 
@@ -266,27 +261,27 @@
 
     def far_send_one(n, value):
         far_out[n] = folded(value)
-        send(far_out.at[n], far_in.at[n], far_send.at[n], far_recv.at[n], mirror)
+        send(far_out.at[n], far_in.at[n], far_send.at[0], far_recv.at[n], mirror)
 
     def with_far(own, n):
-        arrive(far_in.at[n], far_send.at[n], far_recv.at[n], mirror)
+        arrived(far_in.at[n], far_recv.at[n])
         return jnp.concatenate([wide(own), unfolded(far_in[n])], axis=0)
 
     def hop(n, value, to):
         hop_out[n] = value
-        send(hop_out.at[n], hop_in.at[n], hop_send.at[n], hop_recv.at[n], to)
-
-    def hopped(n, to):
-        arrive(hop_in.at[n], hop_send.at[n], hop_recv.at[n], to)
+        send(hop_out.at[n], hop_in.at[n], hop_send.at[0], hop_recv.at[n], to)
+
+    def hopped(n):
+        arrived(hop_in.at[n], hop_recv.at[n])
         return wide(hop_in[n])
 
     def deliver(n, target, period, value):
         mirror_out[n] = folded(value[8:])
-        send(mirror_out.at[n], mirror_in.at[n], mirror_send.at[n], mirror_recv.at[n], mirror)
+        send(mirror_out.at[n], mirror_in.at[n], mirror_send.at[0], mirror_recv.at[n], mirror)
         target[period, 0, 0] = value[:8].astype(BF16)
 
     def delivered(n, target, period):
-        arrive(mirror_in.at[n], mirror_send.at[n], mirror_recv.at[n], mirror)
+        arrived(mirror_in.at[n], mirror_recv.at[n])
         target[period, 1, 0] = unfolded(mirror_in[n]).astype(BF16)
 
     def rounded(value):
@@ -320,10 +315,10 @@
         return jnp.concatenate([wide(pair[0]), wide(pair[1])], axis=0)
 
     def begin_later_forward():
-        begin(FB, jnp.where(s == 0, joined(entering[0]), hopped(0, after)))
+        begin(FB, jnp.where(s == 0, joined(entering[0]), hopped(0)))
 
     def begin_later_grads():
-        begin(GB, jnp.where(s == sections - 1, joined(cot_entering[0]), hopped(1, before)))
+        begin(GB, jnp.where(s == sections - 1, joined(cot_entering[0]), hopped(1)))
 
     def far_saved():
         far_send_one(2, saved[0, 1, 0])
@@ -332,8 +327,12 @@
     def end():
         for n, target in enumerate((states_out, input_grads) * 2):
             delivered(n, target, n // 2)
-        for copy in sends:
-            copy.wait_send()
+        for like, sem in ((far_out, far_send), (hop_out, hop_send), (mirror_out, mirror_send)):
+            departed(like, sem.at[0])
+        for sem, count in ((ag_send, 6), (rs_send, 4)):
+            for n in range(count):
+                departed(blocks[6], sem.at[n, 0])
+                departed(blocks[24], sem.at[n, 1])
 
     chosen = lax.broadcasted_iota(jnp.int32, gains.shape, 0) == s
     gain = jnp.sum(jnp.where(chosen, wide(gains[...]), 0.0), axis=0, keepdims=True)
@@ -420,15 +419,15 @@
             vmem((256, units), BF16),
             vmem((2, 2, units, 256), BF16),
             dma((4,)),
-            dma((6, 2, 9)),
-            dma((6, 2, 9)),
-            dma((4, 2, 9)),
-            dma((4, 2, 9)),
+            dma((6, 2)),
+            dma((6, 3)),
+            dma((4, 2)),
+            dma((4, 3)),
+            dma((1,)),
             dma((4,)),
-            dma((4,)),
+            dma((1,)),
             dma((2,)),
-            dma((2,)),
-            dma((4,)),
+            dma((1,)),
             dma((4,)),
         ],
         compiler_params=pltpu.CompilerParams(

time: 128 us -> 125 us (0.977)
  Pallas kernels: 127 us -> 125 us
    pallas_call x1, Pallas kernels: 124 us -> 121 us  [body(): pl.pallas_call(kernel, out_shape=tuple((vmem(shape, BF16) for shape in sh...]
where the time goes in v5:
time: 125 us
  Pallas kernels  125 us (100%)
    pallas_call x1, Pallas kernels, body(): pl.pallas_call(kernel, out_shape=tuple((vmem(shape, BF16) for shape in sh...  121 us
    pallas_call x1, Pallas kernels, body(): pl.pallas_call(write_out, out_shape=tuple((jax.ShapeDtypeStruct(shape, BF...  3.53 us

profile of v5, /device:TPU:1, one launch (start us, length us, event | category | flops | bytes accessed | tf_op | source)
XLA Modules:
  0.0 125.4 jit_solution(2921060843073030567)
XLA Ops:
  0.6 121.0 %shard_map.111 = (bf16[2,2,1,8,3584]{4,3,2,1,0:T(8,128)(2,1)S(1)}, bf16[2,2,1,8,3584]{4,3,2,1,0:T(8,128)(2,1)S(1)}, bf16[1,576,3584]{2,1,0:T(8,128)(2,1)S(1)}, bf16[1,576,3584]{2,1,0:T(8,128)(2,1)S(1)}) custom-call(bf16[2,1,8,3584]{3,2,1,0:T(8,128)(2,1)} %states_in.1, bf16[1,2,8,3584]{3,2,1,0:T(8,128)(2,1)} %entering.1, bf16[2,2,1,8,3584]{4,3,2,1,0:T(8,128)(2,1)} %saved.1, ...), custom_call_target="tpu_custom_call" | custom-call | flops 15000000512 | bytes 17000000 | tf_op jit(solution)/shard_map/pallas_call | solution.py:395
  121.7 3.5 %shard_map.112 = (bf16[2,2,1,8,3584]{4,3,2,1,0:T(8,128)(2,1)}, bf16[2,2,1,8,3584]{4,3,2,1,0:T(8,128)(2,1)}, bf16[1,576,3584]{2,1,0:T(8,128)(2,1)}, bf16[1,576,3584]{2,1,0:T(8,128)(2,1)}) custom-call(bf16[2,2,1,8,3584]{4,3,2,1,0:T(8,128)(2,1)S(1)} %get-tuple-element.8.refs_0_, bf16[2,2,1,8,3584]{4,3,2,1,0:T(8,128)(2,1)S(1)} %get-tuple-element.9.refs_1_, ...), custom_call_target="tpu_custom_call" | custom-call | tf_op jit(solution)/shard_map/pallas_call | solution.py:438

commit v6 on v5

--- a/solution.py
+++ b/solution.py
@@ -10,16 +10,19 @@
 EPSILON = 1e-06
 MESH = pl.DeviceIdType.MESH
 F32, BF16 = jnp.float32, jnp.bfloat16
-FA, NA, GA, NB, FB, GB = range(6)
-FS, NS, GS = (FA, FB), (NA, NB), (GA, GB)
+D0, D1, GA, NB, FB, GB = range(6)
+NEAR_FORWARD, NEAR_SAVED = 0, 1
+FS, NS, GS = (NEAR_FORWARD, FB), (NEAR_SAVED, NB), (GA, GB)
+PASSED = (GA, NB, D1,)
 RING = 4
 
 ORDER = (
-    "far0", "far1", "far2", "nF0", "nG0", "nN0", "outF0", "outN0", "relF0", "outG0", "relN0",
-    "relG0", "hF0", "pF0h0", "pF0h1", "hB0", "nN1", "gB0", "rsrF0", "pB0h0", "pB0h1", "rsiF0",
-    "rsrB0", "outN1", "finF0", "rsiB0", "nF1", "relN1", "finB0", "outF1", "nG1", "hB1", "relF1",
-    "outG1", "hF1", "relG1", "pF1h0", "pF1h1", "gB1", "rsrF1", "pB1h0", "pB1h1", "w1a", "keepB1",
-    "rsrB1", "rsiF1", "w1b", "keepB0", "rsiB1", "w0a", "finF1", "finB1", "w0b", "end",
+    "far0", "far1", "far2", "nD0", "nD1", "nG0", "outD0", "irD1", "irG0", "relD0", "outD1", "hD0",
+    "relD1", "outG0", "nN1", "hD1", "hF0", "relG0", "pF0h0", "pF0h1", "irN1", "hB0", "gB0",
+    "rsrF0", "pB0h0", "pB0h1", "rsiF0", "rsrB0", "outN1", "finF0", "rsiB0", "nF1", "relN1",
+    "finB0", "outF1", "nG1", "hB1", "relF1", "outG1", "hF1", "relG1", "pF1h0", "pF1h1", "keepB0",
+    "gB1", "rsrF1", "pB1h0", "pB1h1", "keepB1", "w1a", "rsrB1", "rsiF1", "w1b", "rsiB1", "w0a",
+    "finF1", "finB1", "w0b", "end",
 )
 
 
@@ -36,7 +39,7 @@
     states_out, input_grads, grad_up, grad_down,
     up, down, gathered, partial, pass_on, from_prev, from_next, summed, scattered,
     rows, far_out, far_in, hop_out, hop_in, mirror_out, mirror_in,
-    slopes, bent, active, flipped,
+    slopes, bent, active, flipped, near,
     load_sem, ag_send, ag_recv, rs_send, rs_recv, far_send, far_recv,
     hop_send, hop_recv, mirror_send, mirror_recv,
 ):
@@ -101,7 +104,7 @@
             device_id=mirror, device_id_type=MESH,
         ).wait_send()
 
-    blocks = {6: scattered.at[0], 8: from_prev.at[0], 16: from_prev.at[0:2], 24: from_prev.at[0:3]}
+    blocks = {2: from_prev.at[0, 0, 0:2], 4: from_prev.at[0, 0], 6: scattered.at[0], 8: from_prev.at[0], 16: from_prev.at[0:2], 24: from_prev.at[0:3]}
 
     inner, outer = ("x", "z"), ("z", "x")
     low, high, whole = pl.ds(0, half), pl.ds(half, half), pl.ds(0, width)
@@ -116,13 +119,23 @@
         return ref.at[index, h, at["z"], at["x"]]
 
     def gather_inner(a):
-        for step in (1, 3, 2):
+        for step in (1, 3) if a in PASSED else (1, 3, 2):
             for h in range(2):
                 own = block(gathered, a, h, 0)
                 send(own, own, ag_send.at[a, 0], ag_recv.at[a, 0], along(inner[h], step))
 
+    def gather_pass(a):
+        arrived(blocks[4], ag_recv.at[a, 0])
+        for h in range(2):
+            for step, lanes in ((1, low), (-1, high)):
+                passed = block(gathered, a, h, -step).at[:, lanes]
+                send(passed, passed, ag_send.at[a, 0], ag_recv.at[a, 3], along(inner[h], step))
+
     def gather_outer(a):
-        arrived(blocks[6], ag_recv.at[a, 0])
+        if a in PASSED:
+            arrived(blocks[2], ag_recv.at[a, 3])
+        else:
+            arrived(blocks[6], ag_recv.at[a, 0])
         for n, group in ((1, ((1, low), (-1, high))), (2, ((1, high), (-1, low)))):
             for h in range(2):
                 for step, lanes in group:
@@ -220,16 +233,31 @@
                 load.wait()
         return (up, down)[n]
 
+    def pairs(value):
+        return value.reshape(RING * RING, 2, 8, units)
+
+    def hidden_near(direction):
+        gather_end(direction)
+        hidden = pairs(onto_units(direction, weights_of(0)))
+        for n in range(2):
+            near[n, :, direction] = hidden[:, n]
+
     def hidden_forward(period):
-        gather_end(FS[period])
-        hidden = onto_units(FS[period], weights_of(0))
+        if period == 0:
+            hidden = near[0].reshape(-1, units)
+        else:
+            gather_end(FB)
+            hidden = onto_units(FB, weights_of(0))
         active[...] = (hidden * jax.nn.sigmoid(hidden)).astype(BF16)
 
     def hidden_backward(period):
-        gather_end(NS[period])
-        hidden = onto_units(NS[period], weights_of(0))
+        if period == 0:
+            hidden = near[1].reshape(-1, units)
+        else:
+            gather_end(NB)
+            hidden = onto_units(NB, weights_of(0))
         gating = jax.nn.sigmoid(hidden)
-        flipped[1, period] = (hidden * gating).astype(BF16).T
+        flipped[3 + period] = (hidden * gating).astype(BF16).T
         bent[period] = gating * (1.0 + hidden * (1.0 - gating))
 
     def slope(period):
@@ -237,15 +265,22 @@
         slopes[period] = (onto_units(GS[period], weights_of(1)) * bent[period]).astype(BF16)
 
     def keep_slope(period):
-        flipped[0, period] = slopes[period].T
-
-    def weight_grad(kind, h, target, first, second):
+        if period == 1:
+            flipped[2] = slopes[1].T
+            return
+        value = pairs(wide(slopes[0]))
+        for direction in range(2):
+            mine = value[:, direction]
+            mine = jnp.stack([jnp.zeros_like(mine), mine], axis=1).reshape(-1, units)
+            flipped[direction] = mine.astype(BF16).T
+
+    def weight_grad(first, arrays, h, target):
         tile = 256
-        left = jnp.concatenate([flipped[kind, 0], flipped[kind, 1]], axis=1)
+        left = jnp.concatenate([flipped[first + n] for n in range(len(arrays))], axis=1)
         for n in range(width // tile):
             lanes = pl.ds(n * tile, tile)
             right = jnp.concatenate(
-                [gathered[a, h, :, :, :, lanes].reshape(-1, tile) for a in (first, second)], axis=0
+                [gathered[a, h, :, :, :, lanes].reshape(-1, tile) for a in arrays], axis=0
             )
             total = jnp.dot(left, right, preferred_element_type=F32)
             target[0, :, pl.ds(h * width + n * tile, tile)] = total.astype(BF16)
@@ -263,9 +298,12 @@
         far_out[n] = folded(value)
         send(far_out.at[n], far_in.at[n], far_send.at[0], far_recv.at[n], mirror)
 
+    def from_far(n):
+        arrived(far_in.at[n], far_recv.at[n])
+        return unfolded(far_in[n])
+
     def with_far(own, n):
-        arrived(far_in.at[n], far_recv.at[n])
-        return jnp.concatenate([wide(own), unfolded(far_in[n])], axis=0)
+        return jnp.concatenate([wide(own), from_far(n)], axis=0)
 
     def hop(n, value, to):
         hop_out[n] = value
@@ -311,6 +349,13 @@
         put_block(a, value if a in GS else normed(value))
         gather_inner(a)
 
+    def begin_near(direction, forward, kept):
+        own = pl.ds(8 * direction, 8)
+        rows[NEAR_FORWARD, own] = forward
+        rows[NEAR_SAVED, own] = kept
+        put_block(direction, normed(jnp.concatenate([forward, kept], axis=0)))
+        gather_inner(direction)
+
     def joined(pair):
         return jnp.concatenate([wide(pair[0]), wide(pair[1])], axis=0)
 
@@ -320,8 +365,8 @@
     def begin_later_grads():
         begin(GB, jnp.where(s == sections - 1, joined(cot_entering[0]), hopped(1)))
 
-    def far_saved():
-        far_send_one(2, saved[0, 1, 0])
+    def far_rest():
+        far_send_one(2, cotangent[1, 0])
         far_send_one(3, saved[1, 1, 0])
 
     def end():
@@ -338,21 +383,24 @@
     gain = jnp.sum(jnp.where(chosen, wide(gains[...]), 0.0), axis=0, keepdims=True)
     steps = {
         "far0": lambda: far_send_one(0, states_in[1, 0]),
-        "far1": lambda: far_send_one(1, cotangent[1, 0]),
-        "far2": far_saved,
-        "nF0": lambda: begin(FA, with_far(states_in[0, 0], 0)),
-        "nG0": lambda: begin(GA, with_far(cotangent[0, 0], 1)),
-        "nN0": lambda: begin(NA, with_far(saved[0, 0, 0], 2)),
+        "far1": lambda: far_send_one(1, saved[0, 1, 0]),
+        "far2": far_rest,
+        "nD0": lambda: begin_near(D0, wide(states_in[0, 0]), wide(saved[0, 0, 0])),
+        "nD1": lambda: begin_near(D1, from_far(0), from_far(1)),
+        "nG0": lambda: begin(GA, with_far(cotangent[0, 0], 2)),
         "nN1": lambda: begin(NB, with_far(saved[1, 0, 0], 3)),
+        "hD0": lambda: hidden_near(D0),
+        "hD1": lambda: hidden_near(D1),
         "nF1": begin_later_forward,
         "nG1": begin_later_grads,
-        "w1a": lambda: weight_grad(1, 0, grad_down, GA, GB),
-        "w1b": lambda: weight_grad(1, 1, grad_down, GA, GB),
-        "w0a": lambda: weight_grad(0, 0, grad_up, NA, NB),
-        "w0b": lambda: weight_grad(0, 1, grad_up, NA, NB),
+        "w1a": lambda: weight_grad(3, (GA, GB), 0, grad_down),
+        "w1b": lambda: weight_grad(3, (GA, GB), 1, grad_down),
+        "w0a": lambda: weight_grad(0, (D0, D1, NB), 0, grad_up),
+        "w0b": lambda: weight_grad(0, (D0, D1, NB), 1, grad_up),
         "end": end,
     }
-    for a, name in enumerate(("F0", "N0", "G0", "N1", "F1", "G1")):
+    for a, name in enumerate(("D0", "D1", "G0", "N1", "F1", "G1")):
+        steps["ir" + name] = functools.partial(gather_pass, a)
         steps["out" + name] = functools.partial(gather_outer, a)
         steps["rel" + name] = functools.partial(gather_relay, a)
     for period in range(2):
@@ -417,10 +465,11 @@
             vmem((2, 256, units), BF16),
             vmem((2, 256, units), F32),
             vmem((256, units), BF16),
-            vmem((2, 2, units, 256), BF16),
+            vmem((5, units, 256), BF16),
+            vmem((2, 16, 2, 8, units), F32),
             dma((4,)),
             dma((6, 2)),
-            dma((6, 3)),
+            dma((6, 4)),
             dma((4, 2)),
             dma((4, 3)),
             dma((1,)),

time: 125 us -> 123 us (0.984)
  Pallas kernels: 125 us -> 122 us
    pallas_call x1, Pallas kernels: 121 us -> 119 us  [body(): pl.pallas_call(kernel, out_shape=tuple((vmem(shape, BF16) for shape in sh...]
where the time goes in v6:
time: 123 us
  Pallas kernels  122 us (99%)
    pallas_call x1, Pallas kernels, body(): pl.pallas_call(kernel, out_shape=tuple((vmem(shape, BF16) for shape in sh...  119 us
    pallas_call x1, Pallas kernels, body(): pl.pallas_call(write_out, out_shape=tuple((jax.ShapeDtypeStruct(shape, BF...  3.53 us

profile of v6, /device:TPU:1, one launch (start us, length us, event | category | flops | bytes accessed | tf_op | source)
XLA Modules:
  0.0 122.9 jit_solution(7588964503627616705)
XLA Ops:
  0.6 118.5 %shard_map.111 = (bf16[2,2,1,8,3584]{4,3,2,1,0:T(8,128)(2,1)S(1)}, bf16[2,2,1,8,3584]{4,3,2,1,0:T(8,128)(2,1)S(1)}, bf16[1,576,3584]{2,1,0:T(8,128)(2,1)S(1)}, bf16[1,576,3584]{2,1,0:T(8,128)(2,1)S(1)}) custom-call(bf16[2,1,8,3584]{3,2,1,0:T(8,128)(2,1)} %states_in.1, bf16[1,2,8,3584]{3,2,1,0:T(8,128)(2,1)} %entering.1, bf16[2,2,1,8,3584]{4,3,2,1,0:T(8,128)(2,1)} %saved.1, ...), custom_call_target="tpu_custom_call" | custom-call | flops 15000000512 | bytes 17000000 | tf_op jit(solution)/shard_map/pallas_call | solution.py:443
  119.2 3.5 %shard_map.112 = (bf16[2,2,1,8,3584]{4,3,2,1,0:T(8,128)(2,1)}, bf16[2,2,1,8,3584]{4,3,2,1,0:T(8,128)(2,1)}, bf16[1,576,3584]{2,1,0:T(8,128)(2,1)}, bf16[1,576,3584]{2,1,0:T(8,128)(2,1)}) custom-call(bf16[2,2,1,8,3584]{4,3,2,1,0:T(8,128)(2,1)S(1)} %get-tuple-element.8.refs_0_, bf16[2,2,1,8,3584]{4,3,2,1,0:T(8,128)(2,1)S(1)} %get-tuple-element.9.refs_1_, ...), custom_call_target="tpu_custom_call" | custom-call | tf_op jit(solution)/shard_map/pallas_call | solution.py:487

commit v7 on v6

--- a/solution.py
+++ b/solution.py
@@ -13,16 +13,16 @@
 D0, D1, GA, NB, FB, GB = range(6)
 NEAR_FORWARD, NEAR_SAVED = 0, 1
 FS, NS, GS = (NEAR_FORWARD, FB), (NEAR_SAVED, NB), (GA, GB)
-PASSED = (GA, NB, D1,)
+PASSED = (GA, NB, D1, GB,)
 RING = 4
 
 ORDER = (
-    "far0", "far1", "far2", "nD0", "nD1", "nG0", "outD0", "irD1", "irG0", "relD0", "outD1", "hD0",
-    "relD1", "outG0", "nN1", "hD1", "hF0", "relG0", "pF0h0", "pF0h1", "irN1", "hB0", "gB0",
-    "rsrF0", "pB0h0", "pB0h1", "rsiF0", "rsrB0", "outN1", "finF0", "rsiB0", "nF1", "relN1",
-    "finB0", "outF1", "nG1", "hB1", "relF1", "outG1", "hF1", "relG1", "pF1h0", "pF1h1", "keepB0",
-    "gB1", "rsrF1", "pB1h0", "pB1h1", "keepB1", "w1a", "rsrB1", "rsiF1", "w1b", "rsiB1", "w0a",
-    "finF1", "finB1", "w0b", "end",
+    "far0", "far1", "far2", "nD0", "nD1", "outD0", "nG0", "irD1", "relD0", "irG0", "outD1",
+    "relD1", "outG0", "hD0", "hD1", "hF0", "relG0", "pF0h0", "pF0h1", "hB0", "nN1", "gB0", "rsrF0",
+    "pB0h0", "pB0h1", "rsrB0", "rsiF0", "irN1", "rsiB0", "finF0", "outN1", "finB0", "nF1", "relN1",
+    "nG1", "keepB0", "outF1", "hB1", "irG1", "relF1", "outG1", "hF1", "relG1", "pF1h0", "pF1h1",
+    "gB1", "pB1h0", "pB1h1", "keepB1", "w0a", "rsrF1", "rsrB1", "w1a", "w1b", "rsiF1", "rsiB1",
+    "w0b", "finF1", "finB1", "end",
 )
 
 
@@ -38,7 +38,7 @@
     states_in, entering, saved, cotangent, cot_entering, gains, up_rows, down_rows,
     states_out, input_grads, grad_up, grad_down,
     up, down, gathered, partial, pass_on, from_prev, from_next, summed, scattered,
-    rows, far_out, far_in, hop_out, hop_in, mirror_out, mirror_in,
+    split_out, split_in, rows, far_out, far_in, hop_out, hop_in, landed, mirror_out, mirror_in,
     slopes, bent, active, flipped, near,
     load_sem, ag_send, ag_recv, rs_send, rs_recv, far_send, far_recv,
     hop_send, hop_recv, mirror_send, mirror_recv,
@@ -53,20 +53,27 @@
     units = up.shape[1]
     place = {"x": d % RING, "z": (d // RING) * 2 + t}
 
+    far = sections - 1 - s
+
     def device(section, x, z):
         return (section, (z // 2) * RING + x, z % 2)
 
-    def moved(axis, step):
+    def moved(section, axis, step):
         to = dict(place)
         to[axis] = (place[axis] + step) % RING
-        return device(s, to["x"], to["z"])
-
-    neighbours = {(axis, step): moved(axis, step) for axis in "xz" for step in (1, 2, 3)}
+        return device(section, to["x"], to["z"])
+
+    steps_away = [(axis, step) for axis in "xz" for step in (1, 2, 3)]
+    neighbours = {away: moved(s, *away) for away in steps_away}
+    far_neighbours = {away: moved(far, *away) for away in steps_away}
+    mirror = device(far, place["x"], place["z"])
 
     def along(axis, step):
         return neighbours[axis, step % RING]
 
-    mirror = device(sections - 1 - s, place["x"], place["z"])
+    def far_along(axis, step):
+        return far_neighbours[axis, step] if step else mirror
+
     after = device((s + 1) % sections, place["x"], place["z"])
     before = device((s + sections - 1) % sections, place["x"], place["z"])
 
@@ -81,11 +88,9 @@
         load.start()
 
     barrier = pltpu.get_barrier_semaphore()
-    partners = [along(axis, step) for axis in "xz" for step in (1, 2, 3)] + [mirror, after, before]
+    partners = list(neighbours.values()) + list(far_neighbours.values()) + [mirror, after, before]
     for partner in partners:
         pl.semaphore_signal(barrier, inc=1, device_id=partner, device_id_type=MESH)
-    pl.semaphore_wait(barrier, len(partners))
-
     def send(source, target, send_sem, recv_sem, device_id):
         pltpu.make_async_remote_copy(
             src_ref=source, dst_ref=target, send_sem=send_sem, recv_sem=recv_sem,
@@ -176,7 +181,42 @@
                     rs_send.at[p, 1], rs_recv.at[p, 1], along(outer[h], step),
                 )
 
+    def scatter_out(p):
+        arrived(blocks[16], rs_recv.at[p, 1])
+        for h in range(2):
+            total = slab(partial, p, h, 0, whole)[...].astype(F32)
+            total = total + from_prev[p, h].astype(F32) + from_next[p, h].astype(F32)
+            total = total.reshape(RING, 2, 8, width)
+            for direction in range(2):
+                part = total[:, direction]
+                part = jnp.concatenate([part[:, :, :half], part[:, :, half:]], axis=1)
+                split_out[p % 2, h, direction] = part.astype(BF16)
+            for step in (1, 3, 2, 0):
+                at = (place[inner[h]] + step) % RING
+                sems = (rs_send.at[p, 0], rs_recv.at[p, 2])
+                for direction in range(2):
+                    if direction or step:
+                        to = far_along(inner[h], step) if direction else along(inner[h], step)
+                        slot = 3 + step if direction else step - 1
+                        send(split_out.at[p % 2, h, direction, at], split_in.at[p % 2, h, slot], *sems, to)
+
+    def scatter_in(p):
+        arrived(split_in.at[0], rs_recv.at[p, 2])
+        sums = []
+        for direction in range(2):
+            halves = []
+            for h in range(2):
+                parts = [split_in[p % 2, h, slot] for slot in (range(3, 7) if direction else range(3))]
+                if not direction:
+                    parts.append(split_out[p % 2, h, 0, pl.ds(place[inner[h]], 1)][0])
+                total = sum(part.astype(F32) for part in parts)
+                halves += [total[:8], total[8:]]
+            sums.append(jnp.concatenate(halves, axis=1))
+        return sums
+
     def scatter_inner(p):
+        if p >= 2:
+            return scatter_out(p)
         arrived(blocks[16], rs_recv.at[p, 1])
         for h in range(2):
             total = slab(partial, p, h, 0, whole)[...].astype(F32)
@@ -209,6 +249,12 @@
 
     def normed(value):
         return value * factor_of(value) * gain
+
+    def norm_back(own, upstream, scaling, d_normed):
+        scaled = d_normed * scaling
+        factor = factor_of(own)
+        unit = own * factor
+        return upstream + factor * (scaled - unit * mean(unit * scaled))
 
     def tokens(a, h):
         return gathered[a, h].reshape(RING * RING * 16, width)
@@ -294,9 +340,12 @@
     def unfolded(value):
         return jnp.concatenate([wide(value)[:8], wide(value)[8:]], axis=1)
 
+    def far_ready(n):
+        send(far_out.at[n], far_in.at[n], far_send.at[0], far_recv.at[n], mirror)
+
     def far_send_one(n, value):
         far_out[n] = folded(value)
-        send(far_out.at[n], far_in.at[n], far_send.at[0], far_recv.at[n], mirror)
+        far_ready(n)
 
     def from_far(n):
         arrived(far_in.at[n], far_recv.at[n])
@@ -307,11 +356,22 @@
 
     def hop(n, value, to):
         hop_out[n] = value
-        send(hop_out.at[n], hop_in.at[n], hop_send.at[0], hop_recv.at[n], to)
-
-    def hopped(n):
-        arrived(hop_in.at[n], hop_recv.at[n])
-        return wide(hop_in[n])
+
+        @pl.when(s != (0 if n else sections - 1))
+        def _():
+            send(hop_out.at[n], hop_in.at[n], hop_send.at[n], hop_recv.at[n], to)
+
+    def hopped(n, entered, edge):
+        @pl.when(s == edge)
+        def _():
+            landed[...] = joined(entered[0])
+
+        @pl.when(s != edge)
+        def _():
+            arrived(hop_in.at[n], hop_recv.at[n])
+            landed[...] = wide(hop_in[n])
+
+        return landed[...]
 
     def deliver(n, target, period, value):
         mirror_out[n] = folded(value[8:])
@@ -326,23 +386,26 @@
         return wide(value.astype(BF16))
 
     def finish_forward(period):
-        p = 2 * period
-        produced = rounded(rows[FS[period]] + scatter_end(p))
-        if period == 0:
-            hop(0, produced.astype(BF16), after)
-        deliver(p, states_out, period, produced)
+        if period == 1:
+            near_sum, far_sum = scatter_in(2)
+            states_out[1, 0, 0] = (rows[FB, 0:8] + near_sum).astype(BF16)
+            states_out[1, 1, 0] = (from_far(4) + far_sum).astype(BF16)
+            return
+        produced = rounded(rows[NEAR_FORWARD] + scatter_end(0))
+        hop(0, produced.astype(BF16), after)
+        deliver(0, states_out, 0, produced)
 
     def finish_backward(period):
-        p = 2 * period + 1
-        scaled = scatter_end(p) * gain
-        own = rows[NS[period]]
-        factor = factor_of(own)
-        unit = own * factor
-        back = factor * (scaled - unit * mean(unit * scaled))
-        back = rounded(rows[GS[period]] + back)
-        if period == 0:
-            hop(1, back.astype(BF16), before)
-        deliver(p, input_grads, period, back)
+        if period == 1:
+            near_sum, far_sum = scatter_in(3)
+            back = norm_back(rows[NB, 0:8], rows[GB, 0:8], gain, near_sum)
+            input_grads[1, 0, 0] = back.astype(BF16)
+            back = norm_back(wide(saved[1, 1, 0]), from_far(5), far_gain, far_sum)
+            input_grads[1, 1, 0] = back.astype(BF16)
+            return
+        back = rounded(norm_back(rows[NEAR_SAVED], rows[GA], gain, scatter_end(1)))
+        hop(1, back.astype(BF16), before)
+        deliver(1, input_grads, 0, back)
 
     def begin(a, value):
         rows[a] = value
@@ -354,39 +417,56 @@
         rows[NEAR_FORWARD, own] = forward
         rows[NEAR_SAVED, own] = kept
         put_block(direction, normed(jnp.concatenate([forward, kept], axis=0)))
-        gather_inner(direction)
 
     def joined(pair):
         return jnp.concatenate([wide(pair[0]), wide(pair[1])], axis=0)
 
     def begin_later_forward():
-        begin(FB, jnp.where(s == 0, joined(entering[0]), hopped(0)))
+        begin(FB, hopped(0, entering, 0))
+        far_send_one(4, rows[FB, 8:16])
 
     def begin_later_grads():
-        begin(GB, jnp.where(s == sections - 1, joined(cot_entering[0]), hopped(1)))
+        begin(GB, hopped(1, cot_entering, sections - 1))
+        far_send_one(5, rows[GB, 8:16])
+
+    def begin_far():
+        begin_near(D1, from_far(0), from_far(1))
+        gather_inner(D1)
 
     def far_rest():
-        far_send_one(2, cotangent[1, 0])
-        far_send_one(3, saved[1, 1, 0])
+        far_ready(2)
+        far_ready(3)
 
     def end():
-        for n, target in enumerate((states_out, input_grads) * 2):
-            delivered(n, target, n // 2)
-        for like, sem in ((far_out, far_send), (hop_out, hop_send), (mirror_out, mirror_send)):
+        delivered(0, states_out, 0)
+        delivered(1, input_grads, 0)
+        for like, sem in ((far_out, far_send), (mirror_out, mirror_send)):
             departed(like, sem.at[0])
+
+        @pl.when(s != sections - 1)
+        def _():
+            departed(hop_out.at[0], hop_send.at[0])
+
+        @pl.when(s != 0)
+        def _():
+            departed(hop_out.at[1], hop_send.at[1])
+
         for sem, count in ((ag_send, 6), (rs_send, 4)):
             for n in range(count):
-                departed(blocks[6], sem.at[n, 0])
+                departed(split_in.at[0] if sem is rs_send and n >= 2 else blocks[6], sem.at[n, 0])
                 departed(blocks[24], sem.at[n, 1])
 
-    chosen = lax.broadcasted_iota(jnp.int32, gains.shape, 0) == s
-    gain = jnp.sum(jnp.where(chosen, wide(gains[...]), 0.0), axis=0, keepdims=True)
+    def gain_of(layer):
+        chosen = lax.broadcasted_iota(jnp.int32, gains.shape, 0) == layer
+        return jnp.sum(jnp.where(chosen, wide(gains[...]), 0.0), axis=0, keepdims=True)
+
+    gain, far_gain = gain_of(s), gain_of(far)
     steps = {
-        "far0": lambda: far_send_one(0, states_in[1, 0]),
-        "far1": lambda: far_send_one(1, saved[0, 1, 0]),
+        "far0": lambda: far_ready(0),
+        "far1": lambda: far_ready(1),
         "far2": far_rest,
-        "nD0": lambda: begin_near(D0, wide(states_in[0, 0]), wide(saved[0, 0, 0])),
-        "nD1": lambda: begin_near(D1, from_far(0), from_far(1)),
+        "nD0": lambda: gather_inner(D0),
+        "nD1": begin_far,
         "nG0": lambda: begin(GA, with_far(cotangent[0, 0], 2)),
         "nN1": lambda: begin(NB, with_far(saved[1, 0, 0], 3)),
         "hD0": lambda: hidden_near(D0),
@@ -419,6 +499,10 @@
         for n, name in enumerate("FB"):
             steps["rsr" + name + k] = functools.partial(scatter_relay, 2 * period + n)
             steps["rsi" + name + k] = functools.partial(scatter_inner, 2 * period + n)
+    for n, value in enumerate((states_in[1, 0], saved[0, 1, 0], cotangent[1, 0], saved[1, 1, 0])):
+        far_out[n] = folded(value)
+    begin_near(D0, wide(states_in[0, 0]), wide(saved[0, 0, 0]))
+    pl.semaphore_wait(barrier, len(partners))
     for name in ORDER:
         steps[name]()
 
@@ -455,13 +539,16 @@
             vmem((4, 2) + grid_rows[1:], BF16),
             vmem((4, 2) + grid_rows[1:], BF16),
             vmem((4, 2, 3, 16, width), BF16),
+            vmem((2, 2, 2, RING, 16, width // 2), BF16),
+            vmem((2, 2, 7, 16, width // 2), BF16),
             vmem((6, 16, features), F32),
-            vmem((4, 16, width), BF16),
-            vmem((4, 16, width), BF16),
+            vmem((6, 16, width), BF16),
+            vmem((6, 16, width), BF16),
             vmem((2, 16, features), BF16),
             vmem((2, 16, features), BF16),
-            vmem((4, 16, width), BF16),
-            vmem((4, 16, width), BF16),
+            vmem((16, features), F32),
+            vmem((2, 16, width), BF16),
+            vmem((2, 16, width), BF16),
             vmem((2, 256, units), BF16),
             vmem((2, 256, units), F32),
             vmem((256, units), BF16),
@@ -473,11 +560,11 @@
             dma((4, 2)),
             dma((4, 3)),
             dma((1,)),
-            dma((4,)),
+            dma((6,)),
+            dma((2,)),
+            dma((2,)),
             dma((1,)),
             dma((2,)),
-            dma((1,)),
-            dma((4,)),
         ],
         compiler_params=pltpu.CompilerParams(
             collective_id=0, has_side_effects=True, vmem_limit_bytes=48 * 2**20

time: 123 us -> 122 us (level)
  no operation moved by 1% of the time
where the time goes in v7:
time: 122 us
  Pallas kernels  121 us (99%)
    pallas_call x1, Pallas kernels, body(): pl.pallas_call(kernel, out_shape=tuple((vmem(shape, BF16) for shape in sh...  118 us
    pallas_call x1, Pallas kernels, body(): pl.pallas_call(write_out, out_shape=tuple((jax.ShapeDtypeStruct(shape, BF...  3.53 us

profile of v7, /device:TPU:1, one launch (start us, length us, event | category | flops | bytes accessed | tf_op | source)
XLA Modules:
  0.0 122.2 jit_solution(13064517322185214326)
XLA Ops:
  0.6 117.8 %shard_map.111 = (bf16[2,2,1,8,3584]{4,3,2,1,0:T(8,128)(2,1)S(1)}, bf16[2,2,1,8,3584]{4,3,2,1,0:T(8,128)(2,1)S(1)}, bf16[1,576,3584]{2,1,0:T(8,128)(2,1)S(1)}, bf16[1,576,3584]{2,1,0:T(8,128)(2,1)S(1)}) custom-call(bf16[2,1,8,3584]{3,2,1,0:T(8,128)(2,1)} %states_in.1, bf16[1,2,8,3584]{3,2,1,0:T(8,128)(2,1)} %entering.1, bf16[2,2,1,8,3584]{4,3,2,1,0:T(8,128)(2,1)} %saved.1, ...), custom_call_target="tpu_custom_call" | custom-call | flops 15000000512 | bytes 17000000 | tf_op jit(solution)/shard_map/pallas_call | solution.py:527
  118.5 3.5 %shard_map.112 = (bf16[2,2,1,8,3584]{4,3,2,1,0:T(8,128)(2,1)}, bf16[2,2,1,8,3584]{4,3,2,1,0:T(8,128)(2,1)}, bf16[1,576,3584]{2,1,0:T(8,128)(2,1)}, bf16[1,576,3584]{2,1,0:T(8,128)(2,1)}) custom-call(bf16[2,2,1,8,3584]{4,3,2,1,0:T(8,128)(2,1)S(1)} %get-tuple-element.8.refs_0_, bf16[2,2,1,8,3584]{4,3,2,1,0:T(8,128)(2,1)S(1)} %get-tuple-element.9.refs_1_, ...), custom_call_target="tpu_custom_call" | custom-call | tf_op jit(solution)/shard_map/pallas_call | solution.py:574

commit v8 on v7

--- a/solution.py
+++ b/solution.py
@@ -35,12 +35,12 @@
 
 
 def kernel(
-    states_in, entering, saved, cotangent, cot_entering, gains, up_rows, down_rows,
+    states_in_hbm, entering_hbm, saved_hbm, cotangent_hbm, cot_entering_hbm, gains_hbm, up_rows, down_rows,
     states_out, input_grads, grad_up, grad_down,
     up, down, gathered, partial, pass_on, from_prev, from_next, summed, scattered,
     split_out, split_in, rows, far_out, far_in, hop_out, hop_in, landed, mirror_out, mirror_in,
     slopes, bent, active, flipped, near,
-    load_sem, ag_send, ag_recv, rs_send, rs_recv, far_send, far_recv,
+    states_in, entering, saved, cotangent, cot_entering, gains, load_sem, small_sem, ag_send, ag_recv, rs_send, rs_recv, far_send, far_recv,
     hop_send, hop_recv, mirror_send, mirror_recv,
 ):
     s = lax.axis_index("section")
@@ -77,6 +77,19 @@
     after = device((s + 1) % sections, place["x"], place["z"])
     before = device((s + sections - 1) % sections, place["x"], place["z"])
 
+    barrier = pltpu.get_barrier_semaphore()
+    partners = list(neighbours.values()) + list(far_neighbours.values()) + [mirror, after, before]
+    for partner in partners:
+        pl.semaphore_signal(barrier, inc=1, device_id=partner, device_id_type=MESH)
+    small = [
+        pltpu.make_async_copy(source, target, small_sem.at[n])
+        for n, (source, target) in enumerate((
+            (states_in_hbm, states_in), (saved_hbm, saved), (cotangent_hbm, cotangent),
+            (gains_hbm, gains), (entering_hbm, entering), (cot_entering_hbm, cot_entering),
+        ))
+    ]
+    for copy in small:
+        copy.start()
     loads = [
         pltpu.make_async_copy(
             source.at[0, 0, :, pl.ds(h * width, width)], target.at[h], load_sem.at[2 * n + h]
@@ -87,10 +100,6 @@
     for load in loads:
         load.start()
 
-    barrier = pltpu.get_barrier_semaphore()
-    partners = list(neighbours.values()) + list(far_neighbours.values()) + [mirror, after, before]
-    for partner in partners:
-        pl.semaphore_signal(barrier, inc=1, device_id=partner, device_id_type=MESH)
     def send(source, target, send_sem, recv_sem, device_id):
         pltpu.make_async_remote_copy(
             src_ref=source, dst_ref=target, send_sem=send_sem, recv_sem=recv_sem,
@@ -460,6 +469,8 @@
         chosen = lax.broadcasted_iota(jnp.int32, gains.shape, 0) == layer
         return jnp.sum(jnp.where(chosen, wide(gains[...]), 0.0), axis=0, keepdims=True)
 
+    for copy in small:
+        copy.wait()
     gain, far_gain = gain_of(s), gain_of(far)
     steps = {
         "far0": lambda: far_ready(0),
@@ -527,7 +538,7 @@
     results = pl.pallas_call(
         kernel,
         out_shape=tuple(vmem(shape, BF16) for shape in shapes),
-        in_specs=[in_vmem] * 6 + [anywhere] * 2,
+        in_specs=[anywhere] * 8,
         out_specs=(in_vmem,) * 4,
         scratch_shapes=[
             vmem((2, units, width), BF16),
@@ -554,7 +565,14 @@
             vmem((256, units), BF16),
             vmem((5, units, 256), BF16),
             vmem((2, 16, 2, 8, units), F32),
+            vmem(states_in.shape, BF16),
+            vmem(entering.shape, BF16),
+            vmem(saved.shape, BF16),
+            vmem(cotangent.shape, BF16),
+            vmem(cot_entering.shape, BF16),
+            vmem(gains.shape, BF16),
             dma((4,)),
+            dma((6,)),
             dma((6, 2)),
             dma((6, 4)),
             dma((4, 2)),

time: 122 us -> 121 us (level)
    pallas_call x1, Pallas kernels: 118 us -> 117 us  [body(): pl.pallas_call(kernel, out_shape=tuple((vmem(shape, BF16) for shape in sh...]
where the time goes in v8:
time: 121 us
  Pallas kernels  120 us (99%)
    pallas_call x1, Pallas kernels, body(): pl.pallas_call(kernel, out_shape=tuple((vmem(shape, BF16) for shape in sh...  117 us
    pallas_call x1, Pallas kernels, body(): pl.pallas_call(write_out, out_shape=tuple((jax.ShapeDtypeStruct(shape, BF...  3.53 us

profile of v8, /device:TPU:1, one launch (start us, length us, event | category | flops | bytes accessed | tf_op | source)
XLA Modules:
  0.0 120.9 jit_solution(1072006268977981838)
XLA Ops:
  0.6 116.5 %shard_map.111 = (bf16[2,2,1,8,3584]{4,3,2,1,0:T(8,128)(2,1)S(1)}, bf16[2,2,1,8,3584]{4,3,2,1,0:T(8,128)(2,1)S(1)}, bf16[1,576,3584]{2,1,0:T(8,128)(2,1)S(1)}, bf16[1,576,3584]{2,1,0:T(8,128)(2,1)S(1)}) custom-call(bf16[2,1,8,3584]{3,2,1,0:T(8,128)(2,1)} %states_in_hbm.1, bf16[1,2,8,3584]{3,2,1,0:T(8,128)(2,1)} %entering_hbm.1, ...), custom_call_target="tpu_custom_call" | custom-call | flops 15000000512 | bytes 17000000 | tf_op jit(solution)/shard_map/pallas_call | solution.py:538
  117.2 3.5 %shard_map.112 = (bf16[2,2,1,8,3584]{4,3,2,1,0:T(8,128)(2,1)}, bf16[2,2,1,8,3584]{4,3,2,1,0:T(8,128)(2,1)}, bf16[1,576,3584]{2,1,0:T(8,128)(2,1)}, bf16[1,576,3584]{2,1,0:T(8,128)(2,1)}) custom-call(bf16[2,2,1,8,3584]{4,3,2,1,0:T(8,128)(2,1)S(1)} %get-tuple-element.8.refs_0_, bf16[2,2,1,8,3584]{4,3,2,1,0:T(8,128)(2,1)S(1)} %get-tuple-element.9.refs_1_, ...), custom_call_target="tpu_custom_call" | custom-call | tf_op jit(solution)/shard_map/pallas_call | solution.py:592

commit v9 on v8

--- a/solution.py
+++ b/solution.py
@@ -17,12 +17,12 @@
 RING = 4
 
 ORDER = (
-    "far0", "far1", "far2", "nD0", "nD1", "outD0", "nG0", "irD1", "relD0", "irG0", "outD1",
-    "relD1", "outG0", "hD0", "hD1", "hF0", "relG0", "pF0h0", "pF0h1", "hB0", "nN1", "gB0", "rsrF0",
-    "pB0h0", "pB0h1", "rsrB0", "rsiF0", "irN1", "rsiB0", "finF0", "outN1", "finB0", "nF1", "relN1",
-    "nG1", "keepB0", "outF1", "hB1", "irG1", "relF1", "outG1", "hF1", "relG1", "pF1h0", "pF1h1",
-    "gB1", "pB1h0", "pB1h1", "keepB1", "w0a", "rsrF1", "rsrB1", "w1a", "w1b", "rsiF1", "rsiB1",
-    "w0b", "finF1", "finB1", "end",
+    "far0", "far1", "nD0", "nD1", "outD0", "far2", "irD1", "nG0", "relD0", "outD1", "hD0", "irG0",
+    "relD1", "outG0", "hD1", "hF0", "relG0", "pF0h0", "pF0h1", "nN1", "hB0", "gB0", "rsrF0",
+    "pB0h0", "pB0h1", "rsrB0", "rsiF0", "irN1", "rsiB0", "finF0", "outN1", "keepB0", "finB0",
+    "nF1", "relN1", "nG1", "outF1", "irG1", "hB1", "relF1", "outG1", "hF1", "relG1", "pF1h0",
+    "pF1h1", "gB1", "pB1h0", "pB1h1", "keepB1", "rsrF1", "w0a", "w1a", "rsrB1", "w1b", "rsiF1",
+    "rsiB1", "w0b", "finF1", "finB1", "end",
 )
 
 

time: 121 us -> 121 us (level)
  no operation moved by 1% of the time
where the time goes in v9:
time: 121 us
  Pallas kernels  120 us (99%)
    pallas_call x1, Pallas kernels, body(): pl.pallas_call(kernel, out_shape=tuple((vmem(shape, BF16) for shape in sh...  116 us
    pallas_call x1, Pallas kernels, body(): pl.pallas_call(write_out, out_shape=tuple((jax.ShapeDtypeStruct(shape, BF...  3.53 us

profile of v9, /device:TPU:1, one launch (start us, length us, event | category | flops | bytes accessed | tf_op | source)
XLA Modules:
  0.0 120.6 jit_solution(1058165594868992829)
XLA Ops:
  0.6 116.3 %shard_map.111 = (bf16[2,2,1,8,3584]{4,3,2,1,0:T(8,128)(2,1)S(1)}, bf16[2,2,1,8,3584]{4,3,2,1,0:T(8,128)(2,1)S(1)}, bf16[1,576,3584]{2,1,0:T(8,128)(2,1)S(1)}, bf16[1,576,3584]{2,1,0:T(8,128)(2,1)S(1)}) custom-call(bf16[2,1,8,3584]{3,2,1,0:T(8,128)(2,1)} %states_in_hbm.1, bf16[1,2,8,3584]{3,2,1,0:T(8,128)(2,1)} %entering_hbm.1, ...), custom_call_target="tpu_custom_call" | custom-call | flops 15000000512 | bytes 17000000 | tf_op jit(solution)/shard_map/pallas_call | solution.py:538
  116.9 3.5 %shard_map.112 = (bf16[2,2,1,8,3584]{4,3,2,1,0:T(8,128)(2,1)}, bf16[2,2,1,8,3584]{4,3,2,1,0:T(8,128)(2,1)}, bf16[1,576,3584]{2,1,0:T(8,128)(2,1)}, bf16[1,576,3584]{2,1,0:T(8,128)(2,1)}) custom-call(bf16[2,2,1,8,3584]{4,3,2,1,0:T(8,128)(2,1)S(1)} %get-tuple-element.8.refs_0_, bf16[2,2,1,8,3584]{4,3,2,1,0:T(8,128)(2,1)S(1)} %get-tuple-element.9.refs_1_, ...), custom_call_target="tpu_custom_call" | custom-call | tf_op jit(solution)/shard_map/pallas_call | solution.py:592
